TPU v7x, 128 devices: a whole 4x4x4 slice. The times are simulated.
128 devices in a mesh: dp: 8 (over z, core), expert: 16 (over y, x).
Axes of the slice: x: 4, y: 4, z: 4, core: 2. Of those that a mesh axis runs over, the one named last changes fastest.
Arguments:
- tokens: bfloat16 [16384, 2048], P(('dp', 'expert')), may hold values from -6 to 6
- expert_ids: int32 [16384, 8], P(('dp', 'expert')), may hold values from 0 to 127, as said below
- gate_codes: int32 [16384, 8], P(('dp', 'expert')), may hold values from 1 to 255
- grad_out: bfloat16 [16384, 2048], P(('dp', 'expert')), may hold values from -6 to 6
- w_gate: bfloat16 [128, 2048, 768], P('expert', 'dp'), may hold values from -0.125 to 0.125
- w_up: bfloat16 [128, 2048, 768], P('expert', 'dp'), may hold values from -0.125 to 0.125
- w_down: bfloat16 [128, 2048, 768], P('expert', 'dp'), may hold values from -0.21875 to 0.21875
Outputs:
- mixed: bfloat16 [16384, 2048], P(('dp', 'expert'))
- tokens_grad: bfloat16 [16384, 2048], P(('dp', 'expert'))
- w_gate_grad: bfloat16 [128, 2048, 768], P('expert', 'dp')
- w_up_grad: bfloat16 [128, 2048, 768], P('expert', 'dp')
- w_down_grad: bfloat16 [128, 2048, 768], P('expert', 'dp')
Inputs may be any that keep to these rules, and one draw needn't show every extreme that they name: `expert_ids`: each row names 8 different experts. Among the routes of the 128 tokens of one device (aligned blocks of rows), no expert is named more than 16 times, and some expert is named exactly 16 times by the tokens of every device.
All inputs are finite; a program needn't handle non-finite values.
Results may differ from a plain program's by a relative error of at most 0.0064.
Values may be sent and summed in bfloat16 or wider, within the bound.
A program may use at most 256 MiB of HBM per device.

v0:
```python
import math

import jax
import jax.numpy as jnp
from jax import lax
from jax.sharding import PartitionSpec as P


def expert_forward(row_set, gate_weight, up_weight, down_weight):
    gate_pre = jnp.dot(row_set, gate_weight, preferred_element_type=jnp.float32)
    up_pre = jnp.dot(row_set, up_weight, preferred_element_type=jnp.float32)
    hidden = (gate_pre * jax.nn.sigmoid(gate_pre) * up_pre).astype(jnp.bfloat16)
    output = lax.dot_general(
        hidden, down_weight, (((1,), (1,)), ((), ())), preferred_element_type=jnp.float32
    )
    return (output.astype(jnp.bfloat16), gate_pre, up_pre, hidden)


def local_grads(gate_pre, up_pre, upstream, gate_weight, up_weight, down_weight):
    hidden_grad = jnp.dot(upstream, down_weight, preferred_element_type=jnp.float32)
    sigmoid = jax.nn.sigmoid(gate_pre)
    gate_grad = (hidden_grad * up_pre * sigmoid * (1.0 + gate_pre * (1.0 - sigmoid))).astype(
        jnp.bfloat16
    )
    up_grad = (hidden_grad * gate_pre * sigmoid).astype(jnp.bfloat16)
    contract = (((1,), (1,)), ((), ()))
    route_grad = lax.dot_general(
        gate_grad, gate_weight, contract, preferred_element_type=jnp.float32
    )
    route_grad = route_grad + lax.dot_general(
        up_grad, up_weight, contract, preferred_element_type=jnp.float32
    )
    return (route_grad.astype(jnp.bfloat16), gate_grad, up_grad)


def weight_totals(row_set, gate_grad, up_grad, upstream, hidden):
    across = (((0,), (0,)), ((), ()))
    gate_total = lax.dot_general(row_set, gate_grad, across, preferred_element_type=jnp.float32)
    up_total = lax.dot_general(row_set, up_grad, across, preferred_element_type=jnp.float32)
    down_total = lax.dot_general(upstream, hidden, across, preferred_element_type=jnp.float32)
    return (gate_total, up_total, down_total)


def exchange_rows(row_set):
    return lax.all_to_all(row_set, ("dp", "expert"), split_axis=0, concat_axis=0, tiled=True)


def local(tokens, expert_ids, gate_codes, grad_out, w_gate, w_up, w_down):
    dp_size = lax.axis_size("dp")
    ep_size = lax.axis_size("expert")
    device_count = dp_size * ep_size
    tok_dev, route_count = expert_ids.shape
    model_width = tokens.shape[1]
    pair_count = tok_dev * route_count
    slot_cap = 2 * pair_count // device_count
    slot_count = device_count * slot_cap
    zero_row = jnp.zeros((1, model_width), jnp.bfloat16)
    gate_full, up_full, down_full = (
        lax.all_to_all(w_gate, "dp", split_axis=0, concat_axis=1, tiled=True),
        lax.all_to_all(w_up, "dp", split_axis=0, concat_axis=1, tiled=True),
        lax.all_to_all(w_down, "dp", split_axis=0, concat_axis=1, tiled=True),
    )
    gate_full = gate_full[0]
    up_full = up_full[0]
    down_full = down_full[0]
    hidden_width = gate_full.shape[1]
    flat_ids = expert_ids.reshape(-1)
    target = flat_ids % dp_size * ep_size + flat_ids // dp_size
    onehot = (target[:, None] == jnp.arange(device_count, dtype=jnp.int32)[None, :]).astype(
        jnp.int32
    )
    before = jnp.cumsum(onehot, axis=0) - onehot
    slot_rank = jnp.sum(before * onehot, axis=1)
    slot_of = target * slot_cap + slot_rank
    source = (
        jnp.full((slot_count,), pair_count, jnp.int32)
        .at[slot_of]
        .set(jnp.arange(pair_count, dtype=jnp.int32))
    )
    token_of = jnp.where(source < pair_count, source // route_count, tok_dev)
    counts = jnp.sum(onehot, axis=0).astype(jnp.bfloat16).reshape(device_count, 1)
    send_rows = jnp.concatenate([tokens, zero_row])[token_of].reshape(
        device_count, slot_cap, model_width
    )
    arrived, arrived_counts = (
        lax.all_to_all(send_rows, ("dp", "expert"), split_axis=0, concat_axis=0, tiled=True),
        lax.all_to_all(counts, ("dp", "expert"), split_axis=0, concat_axis=0, tiled=True),
    )
    rows_in = arrived.reshape(slot_count, model_width)
    counts_in = arrived_counts.reshape(device_count).astype(jnp.int32)
    gate_values = gate_codes.reshape(-1).astype(jnp.float32) / 256.0
    upstream_pairs = (
        gate_values[:, None] * jnp.repeat(grad_out, route_count, axis=0).astype(jnp.float32)
    ).astype(jnp.bfloat16)
    upstream_send = jnp.concatenate([upstream_pairs, zero_row])[source]
    within = jnp.arange(slot_cap, dtype=jnp.int32)
    offsets = jnp.cumsum(counts_in) - counts_in
    position = jnp.where(
        within[None, :] < counts_in[:, None], offsets[:, None] + within[None, :], slot_count
    ).reshape(-1)
    compact_source = (
        jnp.full((slot_count + 1,), slot_count, jnp.int32)
        .at[position]
        .set(jnp.arange(slot_count, dtype=jnp.int32))[:slot_count]
    )
    used_total = jnp.sum(counts_in)
    block_rows = math.gcd(slot_count, 512)
    block_count = slot_count // block_rows
    packed_rows = jnp.concatenate([rows_in, zero_row])[compact_source]
    block_starts = jnp.arange(block_count, dtype=jnp.int32) * block_rows

    def forward_block(start):

        def forward_run_block(_):
            return expert_forward(
                lax.dynamic_slice_in_dim(packed_rows, start, block_rows, 0),
                gate_full,
                up_full,
                down_full,
            )

        def forward_skip_block(_):
            return (
                jnp.zeros((block_rows, model_width), jnp.bfloat16),
                jnp.zeros((block_rows, hidden_width), jnp.float32),
                jnp.zeros((block_rows, hidden_width), jnp.float32),
                jnp.zeros((block_rows, hidden_width), jnp.bfloat16),
            )

        return lax.cond(start < used_total, forward_run_block, forward_skip_block, 0)

    stacked = lax.map(forward_block, block_starts)
    packed_out = stacked[0].reshape(slot_count, model_width)
    gate_pre = stacked[1]
    up_pre = stacked[2]
    hidden = stacked[3].reshape(slot_count, hidden_width)
    out_slots = jnp.concatenate([packed_out, zero_row])[position]
    returned = exchange_rows(out_slots.reshape(device_count, slot_cap, model_width)).reshape(
        slot_count, model_width
    )
    per_pair = returned[slot_of].astype(jnp.float32)
    mixed_sum = jnp.sum(
        (gate_values[:, None] * per_pair).reshape(tok_dev, route_count, model_width), axis=1
    ).astype(jnp.bfloat16)
    upstream_in = exchange_rows(upstream_send.reshape(device_count, slot_cap, model_width)).reshape(
        slot_count, model_width
    )
    packed_upstream = jnp.concatenate([upstream_in, zero_row])[compact_source]
    upstream_blocks = packed_upstream.reshape(block_count, block_rows, model_width)

    def backward_block(inputs):
        start, gate_piece, up_piece, upstream_piece = inputs

        def backward_run_block(_):
            return local_grads(gate_piece, up_piece, upstream_piece, gate_full, up_full, down_full)

        def backward_skip_block(_):
            return (
                jnp.zeros((block_rows, model_width), jnp.bfloat16),
                jnp.zeros((block_rows, hidden_width), jnp.bfloat16),
                jnp.zeros((block_rows, hidden_width), jnp.bfloat16),
            )

        return lax.cond(start < used_total, backward_run_block, backward_skip_block, 0)

    grads_stacked = lax.map(backward_block, (block_starts, gate_pre, up_pre, upstream_blocks))
    packed_grad = grads_stacked[0].reshape(slot_count, model_width)
    gate_grad = grads_stacked[1].reshape(slot_count, hidden_width)
    up_grad = grads_stacked[2].reshape(slot_count, hidden_width)
    gate_sum, up_sum, down_sum = weight_totals(
        packed_rows, gate_grad, up_grad, packed_upstream, hidden
    )
    grad_slots = jnp.concatenate([packed_grad, zero_row])[position]
    grad_back = exchange_rows(grad_slots.reshape(device_count, slot_cap, model_width)).reshape(
        slot_count, model_width
    )
    grad_pairs = grad_back[slot_of].astype(jnp.float32)
    tokens_grad = jnp.sum(grad_pairs.reshape(tok_dev, route_count, model_width), axis=1).astype(
        jnp.bfloat16
    )
    gate_local, up_local, down_local = (
        lax.all_to_all(
            gate_sum.astype(jnp.bfloat16)[None], "dp", split_axis=1, concat_axis=0, tiled=True
        ),
        lax.all_to_all(
            up_sum.astype(jnp.bfloat16)[None], "dp", split_axis=1, concat_axis=0, tiled=True
        ),
        lax.all_to_all(
            down_sum.astype(jnp.bfloat16)[None], "dp", split_axis=1, concat_axis=0, tiled=True
        ),
    )
    return (mixed_sum, tokens_grad, gate_local, up_local, down_local)


def solution(mesh):
    in_specs = (
        P(("dp", "expert"), None),
        P(("dp", "expert"), None),
        P(("dp", "expert"), None),
        P(("dp", "expert"), None),
        P("expert", "dp", None),
        P("expert", "dp", None),
        P("expert", "dp", None),
    )
    out_specs = (
        P(("dp", "expert"), None),
        P(("dp", "expert"), None),
        P("expert", "dp", None),
        P("expert", "dp", None),
        P("expert", "dp", None),
    )
    return jax.shard_map(local, mesh=mesh, in_specs=in_specs, out_specs=out_specs, check_vma=False)
```

profile of v0, /device:TPU:3, one launch (start us, length us, event | category | flops | bytes accessed | tf_op | source)
XLA Modules:
  0.0 1104.6 jit_solution(1494305001624494558)
XLA Ops:
  4.6 19.1 %all_to_all.89 = bf16[128,1,1]{2,1,0:T(2,128)(2,1)S(1)} all-to-all(bf16[128,1,1]{2,1,0:T(2,128)(2,1)S(1)} %copy.36), channel_id=1, replica_groups=mesh['dp'=8,'expert'=16] {'dp','expert'}, dimensions={0} | all-to-all | bytes 512 | tf_op jit(solution)/shard_map/all_to_all | solution.py:87
  23.8 42.3 %all_to_all.90 = bf16[8,256,768]{2,1,0:T(8,128)(2,1)} all-to-all(bf16[8,256,768]{2,1,0:T(8,128)(2,1)S(1)} %copy-done.2), channel_id=1, replica_groups=mesh['dp'=8,'expert'=16] {'dp'}, dimensions={0} | all-to-all | bytes 6291456 | tf_op jit(solution)/shard_map/all_to_all | solution.py:59
  66.1 42.1 %all_to_all.91 = bf16[8,256,768]{2,1,0:T(8,128)(2,1)} all-to-all(bf16[8,256,768]{2,1,0:T(8,128)(2,1)S(1)} %copy-done.3), channel_id=1, replica_groups=mesh['dp'=8,'expert'=16] {'dp'}, dimensions={0} | all-to-all | bytes 6291456 | tf_op jit(solution)/shard_map/all_to_all | solution.py:60
  118.9 11.0 gather_fusion
  129.9 21.6 %all-to-all-done.4 = bf16[8,256,768]{2,1,0:T(8,128)(2,1)} async-done(((bf16[8,256,768]{2,1,0:T(8,128)(2,1)}), bf16[8,256,768]{2,1,0:T(8,128)(2,1)}, u32[]{:S(2)}, u32[]{:S(2)}) %all-to-all-start.4) | async-done | bytes 3145760 | tf_op jit(solution)/shard_map/all_to_all | solution.py:61
  151.5 6.7 all-to-all-start.1
  161.9 19.1 %gather_fusion.4 = bf16[2048,2048]{1,0:T(8,128)(2,1)} fusion(bf16[1025,2048]{1,0:T(8,128)(2,1)} %concatenate.21, s32[2048]{0:T(1024)S(1)} %get-tuple-element.289), kind=kCustom, calls=%fused_computation.4 | custom fusion | bytes 16785408 | tf_op jit(solution)/shard_map/gather | solution.py:95
  181.0 80.7 %all-to-all-done.1 = bf16[128,16,2048]{2,1,0:T(8,128)(2,1)} async-done(((bf16[128,16,2048]{2,1,0:T(8,128)(2,1)}), bf16[128,16,2048]{2,1,0:T(8,128)(2,1)}, u32[]{:S(2)}, u32[]{:S(2)}) %all-to-all-start.1) | async-done | bytes 8388640 | tf_op jit(solution)/shard_map/all_to_all | solution.py:86
  261.7 8.4 all-to-all-start.6
  273.7 8.1 scatter_custom_fusion.1
  281.8 8.4 concatenate.19
  290.2 21.0 %gather_fusion.1 = bf16[2048,2048]{1,0:T(8,128)(2,1)} fusion(bf16[2049,2048]{1,0:T(8,128)(2,1)} %concatenate.19, s32[2048]{0:T(1024)S(1)} %fusion.35), kind=kCustom, calls=%fused_computation.1 | custom fusion | bytes 16785408 | tf_op jit(solution)/shard_map/gather | solution.py:109
  317.3 89.9 %while.30 = (s32[]{:T(128)}, bf16[4,512,2048]{2,1,0:T(8,128)(2,1)}, f32[4,512,768]{2,1,0:T(8,128)}, f32[4,512,768]{2,1,0:T(8,128)}, bf16[4,512,768]{2,1,0:T(8,12...) while((s32[]{:T(128)}, bf16[4,512,2048]{2,1,0:T(8,128)(2,1)}, ...), condition=%wide.region_11.12_spmd, body=%wide.region_8.11_spmd.sunk | while | flops 4835246080 | bytes 46661940 | solution.py:132
  319.1 16.7 %conditional.4 = (bf16[1,512,2048]{2,1,0:T(8,128)(2,1)S(1)}, f32[1,512,768]{2,1,0:T(8,128)}, f32[1,512,768]{2,1,0:T(8,128)}, bf16[1,512,768]{2,1,0:T(8,128)(2,1)}) conditional(s32[]{:T(128)} %convert_element_type.165, () %tuple.82, (s32[]{:T(128)}, bf16[2048,2048]{1,0:T(8,128)(2,1)}, bf16[2048,768]{1,0:T(8,128)(2,1)}, bf16[2048,768]{1,0:T(8,128)(2,1)}, ...), branch_computations={%region_9.9_spmd, %region_10.10_spmd} | conditional | flops 4835246080 | bytes 34603112 | solution.py:130
  344.9 16.6 %conditional.4 = (bf16[1,512,2048]{2,1,0:T(8,128)(2,1)S(1)}, f32[1,512,768]{2,1,0:T(8,128)}, f32[1,512,768]{2,1,0:T(8,128)}, bf16[1,512,768]{2,1,0:T(8,128)(2,1)}) conditional(s32[]{:T(128)} %convert_element_type.165, () %tuple.82, (s32[]{:T(128)}, bf16[2048,2048]{1,0:T(8,128)(2,1)}, bf16[2048,768]{1,0:T(8,128)(2,1)}, bf16[2048,768]{1,0:T(8,128)(2,1)}, ...), branch_computations={%region_9.9_spmd, %region_10.10_spmd} | conditional | flops 4835246080 | bytes 34603112 | solution.py:130
  370.5 16.6 %conditional.4 = (bf16[1,512,2048]{2,1,0:T(8,128)(2,1)S(1)}, f32[1,512,768]{2,1,0:T(8,128)}, f32[1,512,768]{2,1,0:T(8,128)}, bf16[1,512,768]{2,1,0:T(8,128)(2,1)}) conditional(s32[]{:T(128)} %convert_element_type.165, () %tuple.82, (s32[]{:T(128)}, bf16[2048,2048]{1,0:T(8,128)(2,1)}, bf16[2048,768]{1,0:T(8,128)(2,1)}, bf16[2048,768]{1,0:T(8,128)(2,1)}, ...), branch_computations={%region_9.9_spmd, %region_10.10_spmd} | conditional | flops 4835246080 | bytes 34603112 | solution.py:130
  407.2 8.3 concatenate.22
  415.5 20.8 %gather_fusion.5 = bf16[2048,2048]{1,0:T(8,128)(2,1)} fusion(bf16[2049,2048]{1,0:T(8,128)(2,1)} %concatenate.22, s32[2048]{0:T(1024)S(1)} %fusion.35), kind=kCustom, calls=%fused_computation.5 | custom fusion | bytes 16785408 | tf_op jit(solution)/shard_map/gather | solution.py:148
  444.4 60.2 %while.31 = (s32[]{:T(128)}, bf16[4,512,2048]{2,1,0:T(8,128)(2,1)}, bf16[4,512,768]{2,1,0:T(8,128)(2,1)}, bf16[4,512,768]{2,1,0:T(8,128)(2,1)}, s32[4]{0:T(128)S...) while((s32[]{:T(128)}, bf16[4,512,2048]{2,1,0:T(8,128)(2,1)}, ...), condition=%wide.region_16.17_spmd, body=%wide.region_13.16_spmd.sunk | while | flops 4839047168 | bytes 67111264 | solution.py:166
  446.6 11.8 %conditional.5 = (bf16[1,512,2048]{2,1,0:T(8,128)(2,1)S(1)}, bf16[1,512,768]{2,1,0:T(8,128)(2,1)S(1)}, bf16[1,512,768]{2,1,0:T(8,128)(2,1)}) conditional(s32[]{:T(128)} %convert_element_type.166, () %tuple.86, (bf16[4,512,2048]{2,1,0:T(8,128)(2,1)}, s32[]{:T(128)}, bf16[2048,768]{1,0:T(8,128)(2,1)}, f32[4,512,768]{2,1,0:T(8,128)}, ...), branch_computations={%region_14.14_spmd, %region_15.15_spmd} | conditional | flops 4839047168 | bytes 59769992 | solution.py:164
  446.7 6.5 fusion.18
  464.3 11.8 %conditional.5 = (bf16[1,512,2048]{2,1,0:T(8,128)(2,1)S(1)}, bf16[1,512,768]{2,1,0:T(8,128)(2,1)S(1)}, bf16[1,512,768]{2,1,0:T(8,128)(2,1)}) conditional(s32[]{:T(128)} %convert_element_type.166, () %tuple.86, (bf16[4,512,2048]{2,1,0:T(8,128)(2,1)}, s32[]{:T(128)}, bf16[2048,768]{1,0:T(8,128)(2,1)}, f32[4,512,768]{2,1,0:T(8,128)}, ...), branch_computations={%region_14.14_spmd, %region_15.15_spmd} | conditional | flops 4839047168 | bytes 59769992 | solution.py:164
  481.9 11.8 %conditional.5 = (bf16[1,512,2048]{2,1,0:T(8,128)(2,1)S(1)}, bf16[1,512,768]{2,1,0:T(8,128)(2,1)S(1)}, bf16[1,512,768]{2,1,0:T(8,128)(2,1)}) conditional(s32[]{:T(128)} %convert_element_type.166, () %tuple.86, (bf16[4,512,2048]{2,1,0:T(8,128)(2,1)}, s32[]{:T(128)}, bf16[2048,768]{1,0:T(8,128)(2,1)}, f32[4,512,768]{2,1,0:T(8,128)}, ...), branch_computations={%region_14.14_spmd, %region_15.15_spmd} | conditional | flops 4839047168 | bytes 59769992 | solution.py:164
  481.9 6.5 fusion.18
  504.7 10.2 fusion.23
  514.9 45.1 %copy.54 = bf16[1,2048,768]{2,0,1:T(2,128)(2,1)} copy(bf16[1,2048,768]{2,1,0:T(8,128)(2,1)S(1)} %fusion.23) | data formatting | bytes 6291456 | tf_op jit(solution)/shard_map/broadcast_in_dim | solution.py:183
  560.6 31.6 %reduce.5 = bf16[2048,768]{1,0:T(8,128)(2,1)S(1)} reduce(bf16[2048,1,768]{2,1,0:T(2,128)(2,1)} %bitcast.131, bf16[]{:T(256)} %broadcast.349), dimensions={1}, to_apply=%bitcast.119.reduce_sub_computation | reduce | bytes 6291458
  595.7 28.7 %all-to-all-start.8 = ((bf16[8,2,98304]{2,1,0:T(2,128)(2,1)}), bf16[8,2,98304]{2,1,0:T(2,128)(2,1)S(1)}, u32[]{:S(2)}, u32[]{:S(2)}) async-start(bf16[8,2,98304]{2,1,0:T(2,128)(2,1)} %reshape.475), calls=%async_computation.8 | async-start | bytes 6291456 | tf_op jit(solution)/shard_map/all_to_all | solution.py:182
  624.4 10.2 fusion.24
  634.7 44.7 %copy.53 = bf16[1,2048,768]{2,0,1:T(2,128)(2,1)} copy(bf16[1,2048,768]{2,1,0:T(8,128)(2,1)S(1)} %fusion.24) | data formatting | bytes 6291456 | tf_op jit(solution)/shard_map/broadcast_in_dim | solution.py:186
  679.4 33.2 %reduce.6 = bf16[2048,768]{1,0:T(8,128)(2,1)} reduce(bf16[2048,1,768]{2,1,0:T(2,128)(2,1)} %bitcast.133, bf16[]{:T(256)} %broadcast.349), dimensions={1}, to_apply=%bitcast.118.reduce_sub_computation | reduce | bytes 6291458
  724.1 10.2 fusion.25
  734.4 44.7 %copy.52 = bf16[1,2048,768]{2,0,1:T(2,128)(2,1)} copy(bf16[1,2048,768]{2,1,0:T(8,128)(2,1)S(1)} %fusion.25) | data formatting | bytes 6291456 | tf_op jit(solution)/shard_map/broadcast_in_dim | solution.py:189
  779.1 33.2 %reduce.7 = bf16[2048,768]{1,0:T(8,128)(2,1)} reduce(bf16[2048,1,768]{2,1,0:T(2,128)(2,1)} %bitcast.132, bf16[]{:T(256)} %broadcast.349), dimensions={1}, to_apply=%bitcast.117.reduce_sub_computation | reduce | bytes 6291458
  824.1 8.4 concatenate.20
  832.5 20.8 %gather_fusion.2 = bf16[2048,2048]{1,0:T(8,128)(2,1)} fusion(bf16[2049,2048]{1,0:T(8,128)(2,1)} %concatenate.20, s32[2048]{0:T(1024)S(1)} %broadcast_clamp_fusion), kind=kCustom, calls=%fused_computation.2 | custom fusion | bytes 16785408 | tf_op jit(solution)/shard_map/gather | solution.py:137
  853.3 8.4 all-to-all-done.10
  861.7 8.3 all-to-all-start.5
  870.0 8.4 concatenate.23
  878.3 20.8 %gather_fusion.6 = bf16[2048,2048]{1,0:T(8,128)(2,1)} fusion(bf16[2049,2048]{1,0:T(8,128)(2,1)} %concatenate.23, s32[2048]{0:T(1024)S(1)} %broadcast_clamp_fusion), kind=kCustom, calls=%fused_computation.6 | custom fusion | bytes 16785408 | tf_op jit(solution)/shard_map/gather | solution.py:173
  899.1 74.1 %all-to-all-done.5 = bf16[128,16,2048]{2,1,0:T(8,128)(2,1)} async-done(((bf16[128,16,2048]{2,1,0:T(8,128)(2,1)}), bf16[128,16,2048]{2,1,0:T(8,128)(2,1)}, u32[]{:S(2)}, u32[]{:S(2)}) %all-to-all-start.5) | async-done | bytes 8388640 | tf_op jit(solution)/shard_map/all_to_all | solution.py:45
  973.3 8.8 all-to-all-start.7
  992.4 7.8 reshape.478
  1005.2 7.8 reshape.480
  1017.9 13.3 %gather_fusion.3 = bf16[1024,2048]{1,0:T(8,128)(2,1)} fusion(bf16[2048,2048]{1,0:T(8,128)(2,1)} %bitcast.27, s32[1024]{0:T(1024)S(1)} %broadcast_clamp_fusion.1), kind=kCustom, calls=%fused_computation.3 | custom fusion | bytes 8392704 | tf_op jit(solution)/shard_map/gather | solution.py:141
  1031.2 7.3 fusion.21
  1038.5 46.5 %all-to-all-done.7 = bf16[128,16,2048]{2,1,0:T(8,128)(2,1)} async-done(((bf16[128,16,2048]{2,1,0:T(8,128)(2,1)}), bf16[128,16,2048]{2,1,0:T(8,128)(2,1)}, u32[]{:S(2)}, u32[]{:S(2)}) %all-to-all-start.7) | async-done | bytes 8388640 | tf_op jit(solution)/shard_map/all_to_all | solution.py:45
  1085.1 13.5 %gather_fusion.7 = bf16[1024,2048]{1,0:T(8,128)(2,1)} fusion(bf16[2048,2048]{1,0:T(8,128)(2,1)} %bitcast.35, s32[1024]{0:T(1024)S(1)} %broadcast_clamp_fusion.1), kind=kCustom, calls=%fused_computation.7 | custom fusion | bytes 8392704 | tf_op jit(solution)/shard_map/gather | solution.py:177
  (169 shorter events, 215.5 us)
Async XLA Ops:
  0.6 23.2 %copy-start.2 = (bf16[8,256,768]{2,1,0:T(8,128)(2,1)S(1)}, bf16[8,256,768]{2,1,0:T(8,128)(2,1)}, u32[]{:S(2)}) copy-start(bf16[8,256,768]{2,1,0:T(8,128)(2,1)} %param.19) | copy-start | bytes 9437188
  2.1 0.8 copy-start.7
  23.8 42.3 %copy-start.3 = (bf16[8,256,768]{2,1,0:T(8,128)(2,1)S(1)}, bf16[8,256,768]{2,1,0:T(8,128)(2,1)}, u32[]{:S(2)}) copy-start(bf16[8,256,768]{2,1,0:T(8,128)(2,1)} %param.20) | copy-start | bytes 9437188
  108.2 5.7 copy-start.11
  108.2 43.2 %all-to-all-start.4 = ((bf16[8,256,768]{2,1,0:T(8,128)(2,1)}), bf16[8,256,768]{2,1,0:T(8,128)(2,1)}, u32[]{:S(2)}, u32[]{:S(2)}) async-start(bf16[8,256,768]{2,1,0:T(8,128)(2,1)} %param.21), calls=%async_computation.4 | async-start | bytes 6291456 | tf_op jit(solution)/shard_map/all_to_all | solution.py:61
  114.0 0.6 copy-start.14
  151.5 6.8 copy-start.16
  151.5 6.9 copy-start.10
  151.5 110.2 %all-to-all-start.1 = ((bf16[128,16,2048]{2,1,0:T(8,128)(2,1)}), bf16[128,16,2048]{2,1,0:T(8,128)(2,1)}, u32[]{:S(2)}, u32[]{:S(2)}) async-start(bf16[128,16,2048]{2,1,0:T(8,128)(2,1)} %bitcast.127), calls=%async_computation.1 | async-start | bytes 16777216 | tf_op jit(solution)/shard_map/all_to_all | solution.py:86
  158.4 1.1 copy-start.8
  261.7 145.5 %all-to-all-start.6 = ((bf16[128,16,2048]{2,1,0:T(8,128)(2,1)}), bf16[128,16,2048]{2,1,0:T(8,128)(2,1)}, u32[]{:S(2)}, u32[]{:S(2)}) async-start(bf16[128,16,2048]{2,1,0:T(8,128)(2,1)} %bitcast.125), calls=%async_computation.6 | async-start | bytes 16777216 | tf_op jit(solution)/shard_map/all_to_all | solution.py:45
  273.7 16.5 %copy-start.12 = (s32[2048,1]{0,1:T(1,128)}, s32[2048,1]{0,1:T(1,128)S(1)}, u32[]{:S(2)}) copy-start(s32[2048,1]{0,1:T(1,128)S(1)} %compare_select_fusion) | copy-start | bytes 24580
  320.9 5.6 copy-start.5
  346.6 5.6 copy-start.5
  372.3 5.6 copy-start.5
  446.7 6.5 copy-start.4
  453.2 1.8 copy-start
  453.2 2.2 copy-start.6
  455.4 3.1 copy-start.1
  464.3 6.5 copy-start.4
  470.8 1.8 copy-start
  470.8 2.2 copy-start.6
  473.0 3.1 copy-start.1
  481.9 6.5 copy-start.4
  488.5 1.8 copy-start
  488.5 2.2 copy-start.6
  490.7 3.1 copy-start.1
  595.7 123.4 %all-to-all-start.8 = ((bf16[8,2,98304]{2,1,0:T(2,128)(2,1)}), bf16[8,2,98304]{2,1,0:T(2,128)(2,1)S(1)}, u32[]{:S(2)}, u32[]{:S(2)}) async-start(bf16[8,2,98304]{2,1,0:T(2,128)(2,1)} %reshape.475), calls=%async_computation.8 | async-start | bytes 6291456 | tf_op jit(solution)/shard_map/all_to_all | solution.py:182
  719.0 99.7 %all-to-all-start.9 = ((bf16[8,2,98304]{2,1,0:T(2,128)(2,1)}), bf16[8,2,98304]{2,1,0:T(2,128)(2,1)}, u32[]{:S(2)}, u32[]{:S(2)}) async-start(bf16[8,2,98304]{2,1,0:T(2,128)(2,1)} %reshape.477), calls=%async_computation.9 | async-start | bytes 6291456 | tf_op jit(solution)/shard_map/all_to_all | solution.py:185
  818.7 5.4 copy-start.13
  818.7 43.0 %all-to-all-start.10 = ((bf16[8,2,98304]{2,1,0:T(2,128)(2,1)}), bf16[8,2,98304]{2,1,0:T(2,128)(2,1)}, u32[]{:S(2)}, u32[]{:S(2)}) async-start(bf16[8,2,98304]{2,1,0:T(2,128)(2,1)} %reshape.479), calls=%async_computation.10 | async-start | bytes 6291456 | tf_op jit(solution)/shard_map/all_to_all | solution.py:188
  861.7 111.6 %all-to-all-start.5 = ((bf16[128,16,2048]{2,1,0:T(8,128)(2,1)}), bf16[128,16,2048]{2,1,0:T(8,128)(2,1)}, u32[]{:S(2)}, u32[]{:S(2)}) async-start(bf16[128,16,2048]{2,1,0:T(8,128)(2,1)} %bitcast.128), calls=%async_computation.5 | async-start | bytes 16777216 | tf_op jit(solution)/shard_map/all_to_all | solution.py:45
  973.3 8.8 copy-start.15
  973.3 111.8 %all-to-all-start.7 = ((bf16[128,16,2048]{2,1,0:T(8,128)(2,1)}), bf16[128,16,2048]{2,1,0:T(8,128)(2,1)}, u32[]{:S(2)}, u32[]{:S(2)}) async-start(bf16[128,16,2048]{2,1,0:T(8,128)(2,1)} %bitcast.126), calls=%async_computation.7 | async-start | bytes 16777216 | tf_op jit(solution)/shard_map/all_to_all | solution.py:45
  1017.9 13.3 %copy-start.9 = (f32[128,8]{1,0:T(8,128)S(1)}, f32[128,8]{1,0:T(8,128)}, u32[]{:S(2)}) copy-start(f32[128,8]{1,0:T(8,128)} %copy-done.8) | copy-start | bytes 12292
where the time goes:
time: 1120 us; the launch traced here: 1100 us
  local copies, waits for them, and re-layouts  448 us (40%)
  waiting for transfers between devices  231 us (21%)
  other arithmetic  118 us (11%)
  matrix products  110 us (10%)
  blocking collectives  104 us (9%)
  starting transfers between devices  77 us (7%)
  loops' own time  15.8 us (1%)
    all_to_all x3, waiting for transfers between devices, exchange_rows(): lax.all_to_all(row_set, ('dp', 'expert'), split_axis=0, concat_axis=0, ti...  121 us
    unnamed x3, other arithmetic  98.1 us
    all_to_all x1, waiting for transfers between devices, local(): lax.all_to_all(send_rows, ('dp', 'expert'), split_axis=0, concat_axis=0,...  80.7 us
    unnamed x35, local copies, waits for them, and re-layouts  54.9 us
    broadcast_in_dim x1, local copies, waits for them, and re-layouts, local(): gate_sum.astype(jnp.bfloat16)[None]  45.1 us
    broadcast_in_dim x1, local copies, waits for them, and re-layouts, local(): up_sum.astype(jnp.bfloat16)[None]  44.7 us
    broadcast_in_dim x1, local copies, waits for them, and re-layouts, local(): down_sum.astype(jnp.bfloat16)[None]  44.7 us
    dynamic_update_slice x20, local copies, waits for them, and re-layouts, local(): stacked = lax.map(forward_block, block_starts)  44.4 us
  transfers between devices with their start and end apart: 8, of which 5 were waited for; matrix products, arithmetic and copies ran while one was open for 42% of the time, Pallas kernels for 0%

commit v1 on v0

v1 whole, which is shorter than its diff:
```python
import functools

import jax
import jax.numpy as jnp
from jax import lax
from jax.experimental import pallas as pl
from jax.experimental.pallas import tpu as pltpu
from jax.sharding import PartitionSpec as P

BF16 = jnp.bfloat16
F32 = jnp.float32
MESH = pl.DeviceIdType.MESH
ANY = pl.BlockSpec(memory_space=pl.ANY)
DP = 8
EP = 16
SIDE = 4
CAP = 16
TOK = 128


def column_peer(step):
    me = lax.axis_index("dp")
    z, core = me // 2, me % 2
    dz, flip = step // 2, step % 2
    other = core if flip == 0 else 1 - core
    return ((z + dz) % SIDE) * 2 + other, ((z + SIDE - dz) % SIDE) * 2 + other


def plane_peer(step):
    me = lax.axis_index("expert")
    y, x = me // SIDE, me % SIDE
    dy, dx = step // SIDE, step % SIDE
    ahead = ((y + dy) % SIDE) * SIDE + (x + dx) % SIDE
    behind = ((y + SIDE - dy) % SIDE) * SIDE + (x + SIDE - dx) % SIDE
    return ahead, behind


PLANE_STEPS = (10, 9, 11, 6, 14, 2, 8, 5, 7, 13, 15, 1, 3, 4, 12)
COLUMN_STEPS = (4, 5, 2, 3, 6, 7, 1)


def greet(column, plane):
    barrier = pltpu.get_barrier_semaphore()
    dp, ep = lax.axis_index("dp"), lax.axis_index("expert")
    count = 0
    for step in column:
        pl.semaphore_signal(barrier, inc=1, device_id=(column_peer(step)[0], ep), device_id_type=MESH)
        count += 1
    for step in plane:
        pl.semaphore_signal(barrier, inc=1, device_id=(dp, plane_peer(step)[0]), device_id_type=MESH)
        count += 1
    pl.semaphore_wait(barrier, count)


def to_column(step, src, dst, send, recv):
    return pltpu.make_async_remote_copy(
        src_ref=src, dst_ref=dst, send_sem=send, recv_sem=recv,
        device_id=(column_peer(step)[0], lax.axis_index("expert")), device_id_type=MESH,
    )


def to_plane(step, src, dst, send, recv):
    return pltpu.make_async_remote_copy(
        src_ref=src, dst_ref=dst, send_sem=send, recv_sem=recv,
        device_id=(lax.axis_index("dp"), plane_peer(step)[0]), device_id_type=MESH,
    )


def gather_kernel(tok, grd, meta, tok_all, grd_all, meta_all, send, recv, fsend, frecv, local):
    me = lax.axis_index("dp")
    greet((2, 4, 6, 1), ())
    pairs = ((meta, meta_all), (tok, tok_all), (grd, grd_all))
    copies = []
    for i, (src, dst) in enumerate(pairs):
        for n, step in enumerate((4, 2, 6, 1)):
            copy = to_column(step, src, dst.at[me], send.at[i, n], recv.at[i, n])
            copy.start()
            copies.append(copy)
    locals_ = []
    for i, (src, dst) in enumerate(pairs):
        copy = pltpu.make_async_copy(src, dst.at[me], local.at[i])
        copy.start()
        locals_.append(copy)
    forwards = []
    for i, (src, dst) in enumerate(pairs):
        for n, step in ((1, 2), (2, 6), (0, 4)):
            behind = column_peer(step)[1]
            copies[4 * i + n].wait_recv()
            copy = to_column(1, dst.at[behind], dst.at[behind], fsend.at[i, n], frecv.at[i, n])
            copy.start()
            forwards.append(copy)
    for i in range(3):
        copies[4 * i + 3].wait_recv()
    for copy in copies:
        copy.wait_send()
    for copy in forwards:
        copy.wait()
    for copy in locals_:
        copy.wait()


def gather_column(tok, grd, meta):
    return pl.pallas_call(
        gather_kernel,
        out_shape=[
            jax.ShapeDtypeStruct((DP,) + tok.shape, tok.dtype),
            jax.ShapeDtypeStruct((DP,) + grd.shape, grd.dtype),
            jax.ShapeDtypeStruct((DP,) + meta.shape, meta.dtype),
        ],
        in_specs=[ANY] * 3,
        out_specs=[ANY] * 3,
        scratch_shapes=[
            pltpu.SemaphoreType.DMA((3, 4)),
            pltpu.SemaphoreType.DMA((3, 4)),
            pltpu.SemaphoreType.DMA((3, 3)),
            pltpu.SemaphoreType.DMA((3, 3)),
            pltpu.SemaphoreType.DMA((3,)),
        ],
        compiler_params=pltpu.CompilerParams(collective_id=0, has_side_effects=True),
        name="gather_column",
    )(tok, grd, meta)


def exchange_kernel(outward, a, b, p, q, r, a_out, b_out, p_out, q_out, r_out,
                    psend, precv, csend, crecv, local):
    dp, ep = lax.axis_index("dp"), lax.axis_index("expert")
    greet(COLUMN_STEPS, PLANE_STEPS)

    def plane_ends(src, dst, target, mine):
        if outward:
            return src.at[:, target], dst.at[mine]
        return src.at[target], dst.at[:, mine]

    copies = []
    for n, step in enumerate(COLUMN_STEPS):
        target = column_peer(step)[0]
        for i, (src, dst) in enumerate(((p, p_out), (q, q_out), (r, r_out))):
            copies.append(to_column(step, src.at[target], dst.at[dp], csend.at[i, n], crecv.at[i, n]))
    for i, (src, dst) in enumerate(((a, a_out), (b, b_out))):
        for n, step in enumerate(PLANE_STEPS):
            target = plane_peer(step)[0]
            ends = plane_ends(src, dst, target, ep)
            copies.append(to_plane(step, *ends, psend.at[i, n], precv.at[i, n]))
    for i, (src, dst) in enumerate(((p, p_out), (q, q_out), (r, r_out))):
        copies.append(pltpu.make_async_copy(src.at[dp], dst.at[dp], local.at[i]))
    for i, (src, dst) in enumerate(((a, a_out), (b, b_out))):
        copies.append(pltpu.make_async_copy(*plane_ends(src, dst, ep, ep), local.at[3 + i]))
    for copy in copies:
        copy.start()
    for copy in copies:
        copy.wait()


def exchange(outward, number, a, b, p, q, r):
    width = a.shape[-1]
    rows = (EP, DP, CAP, width) if outward else (DP, EP, CAP, width)
    return pl.pallas_call(
        functools.partial(exchange_kernel, outward),
        out_shape=[jax.ShapeDtypeStruct(rows, BF16)] * 2 + [jax.ShapeDtypeStruct(p.shape, BF16)] * 3,
        in_specs=[ANY] * 5,
        out_specs=[ANY] * 5,
        scratch_shapes=[
            pltpu.SemaphoreType.DMA((2, EP - 1)),
            pltpu.SemaphoreType.DMA((2, EP - 1)),
            pltpu.SemaphoreType.DMA((3, DP - 1)),
            pltpu.SemaphoreType.DMA((3, DP - 1)),
            pltpu.SemaphoreType.DMA((5,)),
        ],
        compiler_params=pltpu.CompilerParams(collective_id=number, has_side_effects=True),
        name=f"exchange_{number}",
    )(a, b, p, q, r)


def scatter_kernel(a, b, a_out, b_out, own, other, summed, xsend, xrecv, zsend, zrecv, local):
    me = lax.axis_index("dp")
    z, core = me // 2, me % 2
    greet((2, 4, 6, 1), ())
    pairs = ((a, a_out), (b, b_out))
    first, kept = [], []
    for i, (src, _) in enumerate(pairs):
        copy = to_column(1, src.at[:, 1 - core], other.at[i], xsend.at[i], xrecv.at[i])
        copy.start()
        first.append(copy)
        copy = pltpu.make_async_copy(src.at[:, core], own.at[i], local.at[i])
        copy.start()
        kept.append(copy)
    last = []
    for i, (_, dst) in enumerate(pairs):
        first[i].wait_recv()
        kept[i].wait()
        for part in range(SIDE):
            summed[i, part] = (own[i, part].astype(F32) + other[i, part].astype(F32)).astype(BF16)
        for n, step in enumerate((4, 2, 6)):
            copy = to_column(step, summed.at[i, (z + step // 2) % SIDE], dst.at[n], zsend.at[i, n], zrecv.at[i, n])
            copy.start()
            last.append(copy)
        copy = pltpu.make_async_copy(summed.at[i, z], dst.at[3], local.at[2 + i])
        copy.start()
        last.append(copy)
    for copy in last:
        copy.wait()
    for copy in first:
        copy.wait_send()


def scatter_column(a, b):
    _, tok, width = a.shape
    a, b = (v.reshape(SIDE, 2, tok, width) for v in (a, b))
    return pl.pallas_call(
        scatter_kernel,
        out_shape=[jax.ShapeDtypeStruct((SIDE, tok, width), BF16)] * 2,
        in_specs=[ANY] * 2,
        out_specs=[ANY] * 2,
        scratch_shapes=[pltpu.VMEM((2, SIDE, tok, width), BF16)] * 3
        + [
            pltpu.SemaphoreType.DMA((2,)),
            pltpu.SemaphoreType.DMA((2,)),
            pltpu.SemaphoreType.DMA((2, 3)),
            pltpu.SemaphoreType.DMA((2, 3)),
            pltpu.SemaphoreType.DMA((4,)),
        ],
        compiler_params=pltpu.CompilerParams(
            collective_id=3, has_side_effects=True, vmem_limit_bytes=40 * 2**20
        ),
        name="scatter_column",
    )(a, b)


NT = (((1,), (1,)), ((), ()))
TN = (((0,), (0,)), ((), ()))


def dot(a, b, dims=(((1,), (0,)), ((), ()))):
    return lax.dot_general(a, b, dims, preferred_element_type=F32)


def rows_kernel(x, u, wg, wu, wd, out, rg, hid, gg, ug):
    gate, up = dot(x[...], wg[...]), dot(x[...], wu[...])
    s = jax.nn.sigmoid(gate)
    hidden = (gate * s * up).astype(BF16)
    hid[...] = hidden
    out[...] = dot(hidden, wd[...], NT).astype(BF16)
    hg = dot(u[...], wd[...])
    gate_grad = (hg * up * s * (1.0 + gate * (1.0 - s))).astype(BF16)
    up_grad = (hg * gate * s).astype(BF16)
    gg[...] = gate_grad
    ug[...] = up_grad
    rg[...] = (dot(gate_grad, wg[...], NT) + dot(up_grad, wu[...], NT)).astype(BF16)


def expert_rows(x, u, wg, wu, wd):
    rows, width = x.shape
    ff = wg.shape[1]
    block = 256
    wide = pl.BlockSpec((block, width), lambda i: (i, 0))
    thin = pl.BlockSpec((block, ff), lambda i: (i, 0))
    weight = pl.BlockSpec((width, ff), lambda i: (0, 0), pipeline_mode=pl.Buffered(1))
    return pl.pallas_call(
        rows_kernel,
        grid=(rows // block,),
        out_shape=[jax.ShapeDtypeStruct((rows, width), BF16)] * 2
        + [jax.ShapeDtypeStruct((rows, ff), BF16)] * 3,
        in_specs=[wide, wide, weight, weight, weight],
        out_specs=[wide, wide, thin, thin, thin],
        compiler_params=pltpu.CompilerParams(vmem_limit_bytes=56 * 2**20),
        name="expert_rows",
    )(x, u, wg, wu, wd)


def weights_kernel(x, u, hid, gg, ug, dg, du, dd):
    dg[...] = dot(x[...], gg[...], TN).astype(BF16)
    du[...] = dot(x[...], ug[...], TN).astype(BF16)
    dd[...] = dot(u[...], hid[...], TN).astype(BF16)


def expert_weights(x, u, hid, gg, ug):
    rows, width = x.shape
    ff = hid.shape[1]
    block = 256
    slab = pl.BlockSpec((rows, block), lambda i: (0, i))
    whole = pl.BlockSpec((rows, ff), lambda i: (0, 0), pipeline_mode=pl.Buffered(1))
    result = pl.BlockSpec((block, ff), lambda i: (i, 0))
    return pl.pallas_call(
        weights_kernel,
        grid=(width // block,),
        out_shape=[jax.ShapeDtypeStruct((width, ff), BF16)] * 3,
        in_specs=[slab, slab, whole, whole, whole],
        out_specs=[result] * 3,
        compiler_params=pltpu.CompilerParams(vmem_limit_bytes=56 * 2**20),
        name="expert_weights",
    )(x, u, hid, gg, ug)


def local(tokens, expert_ids, gate_codes, grad_out, w_gate, w_up, w_down):
    dp = lax.axis_index("dp")
    tok, width = tokens.shape
    ff = w_gate.shape[-1]
    meta = (expert_ids * 256 + gate_codes).T
    tok_all, grd_all, meta_all = gather_column(tokens, grad_out, meta)
    ids, codes = meta_all // 256, meta_all % 256
    mine = jnp.arange(EP, dtype=jnp.int32) * DP + dp
    named = ids[:, None] == mine[None, :, None, None]
    has = jnp.any(named, axis=2)
    gate = jnp.sum(jnp.where(named, codes[:, None], 0), axis=2).astype(F32) / 256.0
    earlier = jnp.triu(jnp.ones((tok, tok), BF16), 1)
    rank = jnp.dot(has.astype(BF16), earlier, preferred_element_type=F32).astype(jnp.int32)
    slot = jnp.where(has, rank, -1)[:, :, None, :]
    pick = slot == jnp.arange(CAP, dtype=jnp.int32)[None, None, :, None]
    weight = jnp.where(pick, gate[:, :, None, :], 0.0).astype(BF16).reshape(DP, EP * CAP, tok)
    pick = pick.astype(BF16).reshape(DP, EP * CAP, tok)
    gathers = (((2,), (1,)), ((0,), (0,)))
    sends = (((1,), (1,)), ((0,), (0,)))

    def spread(matrix, rows):
        picked = lax.dot_general(matrix, rows, gathers, preferred_element_type=F32)
        return picked.astype(BF16).reshape(DP, EP, CAP, width)

    def collect(matrix, rows):
        summed = lax.dot_general(
            matrix, rows.reshape(DP, EP * CAP, width), sends, preferred_element_type=F32
        )
        return summed.astype(BF16)

    x, u, wg, wu, wd = exchange(
        True, 1, spread(pick, tok_all), spread(weight, grd_all), w_gate, w_up, w_down
    )
    x, u = x.reshape(-1, width), u.reshape(-1, width)
    wg, wu, wd = (w.reshape(width, ff) for w in (wg, wu, wd))
    out, rg, hid, gg, ug = expert_rows(x, u, wg, wu, wd)
    grads = expert_weights(x, u, hid, gg, ug)
    shape = (EP, DP, CAP, width)
    out, rg, dg, du, dd = exchange(
        False, 2, out.reshape(shape), rg.reshape(shape), *(g.reshape(DP, -1, ff) for g in grads)
    )
    mixed, tokens_grad = scatter_column(collect(weight, out), collect(pick, rg))
    mixed, tokens_grad = (
        jnp.sum(v.astype(F32), axis=0).astype(BF16) for v in (mixed, tokens_grad)
    )
    return mixed, tokens_grad, dg, du, dd


def solution(mesh):
    rows, weights = P(("dp", "expert"), None), P("expert", "dp", None)
    return jax.shard_map(
        local,
        mesh=mesh,
        in_specs=(rows,) * 4 + (weights,) * 3,
        out_specs=(rows,) * 2 + (weights,) * 3,
        check_vma=False,
    )
```

time: 1120 us -> 685 us (0.61); the launches traced: 1100 us -> 682 us
  Pallas kernels: 0 us -> 643 us
  local copies, waits for them, and re-layouts: 448 us -> 11 us
  waiting for transfers between devices: 231 us -> 0 us
  other arithmetic: 118 us -> 7.2 us
  blocking collectives: 104 us -> 0 us
  matrix products: 110 us -> 19.8 us
  starting transfers between devices: 77 us -> 0 us
  loops' own time: 15.8 us -> 0 us
    pallas_call x0 -> x6, Pallas kernels: none -> 643 us  [the longest x2 452 us: exchange(): pl.pallas_call(functools.partial(exchange_kernel, outward), out_shape=[ja...]
    all_to_all x8 -> x0, waiting for transfers between devices: 231 us -> none  [the longest x3 121 us: exchange_rows(): lax.all_to_all(row_set, ('dp', 'expert'), split_axis=0, concat_axis=0, ti...]
    gather x8 -> x0, local copies, waits for them, and re-layouts: 140 us -> none  [the longest x1 21 us: local(): packed_rows = jnp.concatenate([rows_in, zero_row])[compact_source]]
    broadcast_in_dim x10 -> x0, local copies, waits for them, and re-layouts: 139 us -> none  [the longest x1 45.1 us: local(): gate_sum.astype(jnp.bfloat16)[None]]
    all_to_all x3 -> x0, blocking collectives: 104 us -> none  [the longest x1 42.3 us: local(): lax.all_to_all(w_gate, 'dp', split_axis=0, concat_axis=1, tiled=True)]
    unnamed x3 -> x1, other arithmetic: 98.1 us -> 0.01 us
    dot_general x21 -> x5, matrix products: 110 us -> 19.8 us  [the longest x2 13.4 us: spread(): picked = lax.dot_general(matrix, rows, gathers, preferred_element_type=F32)]
    all_to_all x8 -> x0, starting transfers between devices: 77 us -> none  [the longest x1 28.7 us: local(): lax.all_to_all(gate_sum.astype(jnp.bfloat16)[None], 'dp', split_axis=1, c...]
  transfers between devices with their start and end apart: 8 -> 0, of which waited for: 5 -> 0; matrix products, arithmetic and copies ran while one was open for 42% -> 0% of each run, Pallas kernels for 0% -> 0%
where the time goes in v1:
time: 685 us; the launch traced here: 682 us
  Pallas kernels  643 us (94%)
  matrix products  19.8 us (3%)
  local copies, waits for them, and re-layouts  11 us (2%)
  other arithmetic  7.2 us (1%)
    pallas_call x2, Pallas kernels, exchange(): pl.pallas_call(functools.partial(exchange_kernel, outward), out_shape=[ja...  452 us
    pallas_call x1, Pallas kernels, scatter_column(): pl.pallas_call(scatter_kernel, out_shape=[jax.ShapeDtypeStruct((SIDE, tok...  55.7 us
    pallas_call x1, Pallas kernels, gather_column(): pl.pallas_call(gather_kernel, out_shape=[jax.ShapeDtypeStruct((DP,) + tok...  55.2 us
    pallas_call x1, Pallas kernels, expert_rows(): pl.pallas_call(rows_kernel, grid=(rows // block,), out_shape=[jax.ShapeDt...  53.2 us
    pallas_call x1, Pallas kernels, expert_weights(): pl.pallas_call(weights_kernel, grid=(width // block,), out_shape=[jax.Sha...  26.6 us

profile of v1, /device:TPU:3, one launch (start us, length us, event | category | flops | bytes accessed | tf_op | source)
XLA Modules:
  0.0 681.7 jit_solution(3557614455091945657)
XLA Ops:
  0.6 1.3 add_bitcast_fusion.meta
  1.9 55.2 %gather_column.1 = (bf16[8,128,2048]{2,1,0:T(8,128)(2,1)}, bf16[8,128,2048]{2,1,0:T(8,128)(2,1)}, s32[8,8,128]{2,1,0:T(8,128)}) custom-call(bf16[128,2048]{1,0:T(8,128)(2,1)} %tok.1, bf16[128,2048]{1,0:T(8,128)(2,1)} %grd.1, s32[8,128]{1,0:T(8,128)} %add_bitcast_fusion.meta), custom_call_target="tpu_custom_call" | custom-call | tf_op jit(solution)/shard_map/gather_column/pallas_call | solution.py:103
  57.1 0.8 add_select_fusion.1
  57.9 0.2 fusion.2
  58.2 0.1 eq.42
  58.3 0.2 compare_reduce_fusion
  58.5 0.1 fusion
  58.7 0.2 fusion.1
  58.9 0.2 bitcast_compare_fusion
  59.1 0.0 copy-start.1
  59.1 7.9 %convolution_convert_fusion.1 = bf16[8,256,2048]{2,1,0:T(8,128)(2,1)} fusion(pred[8,256,128]{2,1,0:T(32,128)(4,1)S(1)} %bitcast_compare_fusion, bf16[8,128,2048]{2,1,0:T(8,128)(2,1)} %get-tuple-element.29), kind=kOutput, calls=%fused_computation.1 | convolution fusion | flops 1077936128 | bytes 12845056 | tf_op jit(solution)/shard_map/dot_general | solution.py:315
  67.0 0.0 copy-done.1
  67.0 5.6 convolution_convert_fusion
  72.6 226.9 %exchange_1.1 = (bf16[16,8,16,2048]{3,2,1,0:T(8,128)(2,1)}, bf16[16,8,16,2048]{3,2,1,0:T(8,128)(2,1)}, bf16[8,256,768]{2,1,0:T(8,128)(2,1)}, bf16[8,256,768]{2,1,0:T(8,128)(2,1)}, bf16[8,256,768]{2,1,0:T(8,128)(2,1)}) custom-call(bf16[8,16,16,2048]{3,2,1,0:T(8,128)(2,1)} %bitcast.44, bf16[8,16,16,2048]{3,2,1,0:T(8,128)(2,1)} %bitcast.45, ...), custom_call_target="tpu_custom_call" | custom-call | tf_op jit(solution)/shard_map/exchange_1/pallas_call | solution.py:157
  299.4 53.2 %expert_rows.1 = (bf16[2048,2048]{1,0:T(8,128)(2,1)}, bf16[2048,2048]{1,0:T(8,128)(2,1)}, bf16[2048,768]{1,0:T(8,128)(2,1)}, bf16[2048,768]{1,0:T(8,128)(2,1)}, bf16[2048,768]{1,0:T(8,128)(2,1)}) custom-call(bf16[2048,2048]{1,0:T(8,128)(2,1)} %bitcast.40, bf16[2048,2048]{1,0:T(8,128)(2,1)} %bitcast.42, bf16[2048,768]{1,0:T(8,128)(2,1)} %bitcast.55, ...), custom_call_target="tpu_custom_call" | custom-call | tf_op jit(solution)/shard_map/expert_rows/pallas_call | solution.py:258
  352.6 26.6 %expert_weights.1 = (bf16[2048,768]{1,0:T(8,128)(2,1)}, bf16[2048,768]{1,0:T(8,128)(2,1)}, bf16[2048,768]{1,0:T(8,128)(2,1)}) custom-call(bf16[2048,2048]{1,0:T(8,128)(2,1)} %bitcast.41, bf16[2048,2048]{1,0:T(8,128)(2,1)} %bitcast.43, bf16[2048,768]{1,0:T(8,128)(2,1)} %get-tuple-element.38.hid, bf16[2048,768]{1,0:T(8,128)(2,1)} %get-tuple-element.39.gg, ...), custom_call_target="tpu_custom_call" | custom-call | tf_op jit(solution)/shard_map/expert_weights/pallas_call | solution.py:283
  379.2 225.3 %exchange_2.1 = (bf16[8,16,16,2048]{3,2,1,0:T(8,128)(2,1)}, bf16[8,16,16,2048]{3,2,1,0:T(8,128)(2,1)}, bf16[8,256,768]{2,1,0:T(8,128)(2,1)}, bf16[8,256,768]{2,1,0:T(8,128)(2,1)}, bf16[8,256,768]{2,1,0:T(8,128)(2,1)}) custom-call(bf16[16,8,16,2048]{3,2,1,0:T(8,128)(2,1)} %bitcast.50, bf16[16,8,16,2048]{3,2,1,0:T(8,128)(2,1)} %bitcast.51, ...), custom_call_target="tpu_custom_call" | custom-call | tf_op jit(solution)/shard_map/exchange_2/pallas_call | solution.py:157
  604.6 0.0 slice-start
  604.6 0.0 slice-start.1
  604.6 4.9 convolution_convert_fusion.3
  609.4 0.0 slice-done
  609.4 1.0 slice-done.1
  610.4 1.4 convolution_convert_fusion.2
  611.8 55.7 %scatter_column.1 = (bf16[4,128,2048]{2,1,0:T(8,128)(2,1)S(1)}, bf16[4,128,2048]{2,1,0:T(8,128)(2,1)S(1)}) custom-call(bf16[4,2,128,2048]{3,2,1,0:T(8,128)(2,1)S(1)} %bitcast.38, bf16[4,2,128,2048]{3,2,1,0:T(8,128)(2,1)S(1)} %bitcast.39), custom_call_target="tpu_custom_call" | custom-call | tf_op jit(solution)/shard_map/scatter_column/pallas_call | solution.py:209
  667.5 0.0 copy-start
  667.5 1.3 copy-done
  668.8 2.9 reduce_sum.34
  671.8 1.3 reduce_sum.35
  673.1 0.0 copy-start.3
  673.1 3.9 copy.27
  677.0 0.0 copy-done.3
  677.0 0.0 copy-start.2
  677.0 1.7 copy.28
  678.6 1.4 copy-done.2
  680.0 1.7 copy.29
  (4 shorter events, 0.0 us)
Async XLA Ops:
  59.1 7.9 %copy-start.1 = (bf16[8,128,2048]{2,1,0:T(8,128)(2,1)S(1)}, bf16[8,128,2048]{2,1,0:T(8,128)(2,1)}, u32[]{:S(2)}) copy-start(bf16[8,128,2048]{2,1,0:T(8,128)(2,1)} %get-tuple-element.30) | copy-start | bytes 12582916
  604.6 4.9 slice-start
  604.6 5.8 slice-start.1
  667.5 1.3 copy-start
  673.1 3.9 copy-start.3
  677.0 3.0 copy-start.2

commit v2 on v1

--- a/solution.py
+++ b/solution.py
@@ -1,5 +1,3 @@
-import functools
-
 import jax
 import jax.numpy as jnp
 from jax import lax
@@ -35,7 +33,7 @@
     return ahead, behind
 
 
-PLANE_STEPS = (10, 9, 11, 6, 14, 2, 8, 5, 7, 13, 15, 1, 3, 4, 12)
+PLANE_STEPS = (10, 5, 15, 7, 13, 6, 14, 9, 11, 2, 8, 1, 3, 4, 12)
 COLUMN_STEPS = (4, 5, 2, 3, 6, 7, 1)
 
 
@@ -121,16 +119,10 @@
     )(tok, grd, meta)
 
 
-def exchange_kernel(outward, a, b, p, q, r, a_out, b_out, p_out, q_out, r_out,
+def exchange_kernel(a, b, p, q, r, a_out, b_out, p_out, q_out, r_out,
                     psend, precv, csend, crecv, local):
     dp, ep = lax.axis_index("dp"), lax.axis_index("expert")
     greet(COLUMN_STEPS, PLANE_STEPS)
-
-    def plane_ends(src, dst, target, mine):
-        if outward:
-            return src.at[:, target], dst.at[mine]
-        return src.at[target], dst.at[:, mine]
-
     copies = []
     for n, step in enumerate(COLUMN_STEPS):
         target = column_peer(step)[0]
@@ -139,35 +131,29 @@
     for i, (src, dst) in enumerate(((a, a_out), (b, b_out))):
         for n, step in enumerate(PLANE_STEPS):
             target = plane_peer(step)[0]
-            ends = plane_ends(src, dst, target, ep)
-            copies.append(to_plane(step, *ends, psend.at[i, n], precv.at[i, n]))
+            copies.append(to_plane(step, src.at[:, target], dst.at[ep], psend.at[i, n], precv.at[i, n]))
     for i, (src, dst) in enumerate(((p, p_out), (q, q_out), (r, r_out))):
         copies.append(pltpu.make_async_copy(src.at[dp], dst.at[dp], local.at[i]))
     for i, (src, dst) in enumerate(((a, a_out), (b, b_out))):
-        copies.append(pltpu.make_async_copy(*plane_ends(src, dst, ep, ep), local.at[3 + i]))
+        copies.append(pltpu.make_async_copy(src.at[:, ep], dst.at[ep], local.at[3 + i]))
     for copy in copies:
         copy.start()
     for copy in copies:
         copy.wait()
 
 
-def exchange(outward, number, a, b, p, q, r):
+def exchange(a, b, p, q, r):
     width = a.shape[-1]
-    rows = (EP, DP, CAP, width) if outward else (DP, EP, CAP, width)
+    dma = pltpu.SemaphoreType.DMA
     return pl.pallas_call(
-        functools.partial(exchange_kernel, outward),
-        out_shape=[jax.ShapeDtypeStruct(rows, BF16)] * 2 + [jax.ShapeDtypeStruct(p.shape, BF16)] * 3,
+        exchange_kernel,
+        out_shape=[jax.ShapeDtypeStruct((EP, DP, CAP, width), BF16)] * 2
+        + [jax.ShapeDtypeStruct(p.shape, BF16)] * 3,
         in_specs=[ANY] * 5,
         out_specs=[ANY] * 5,
-        scratch_shapes=[
-            pltpu.SemaphoreType.DMA((2, EP - 1)),
-            pltpu.SemaphoreType.DMA((2, EP - 1)),
-            pltpu.SemaphoreType.DMA((3, DP - 1)),
-            pltpu.SemaphoreType.DMA((3, DP - 1)),
-            pltpu.SemaphoreType.DMA((5,)),
-        ],
-        compiler_params=pltpu.CompilerParams(collective_id=number, has_side_effects=True),
-        name=f"exchange_{number}",
+        scratch_shapes=[dma((2, EP - 1)), dma((2, EP - 1)), dma((3, DP - 1)), dma((3, DP - 1)), dma((5,))],
+        compiler_params=pltpu.CompilerParams(collective_id=1, has_side_effects=True),
+        name="exchange",
     )(a, b, p, q, r)
 
 
@@ -234,61 +220,214 @@
     return lax.dot_general(a, b, dims, preferred_element_type=F32)
 
 
-def rows_kernel(x, u, wg, wu, wd, out, rg, hid, gg, ug):
-    gate, up = dot(x[...], wg[...]), dot(x[...], wu[...])
-    s = jax.nn.sigmoid(gate)
-    hidden = (gate * s * up).astype(BF16)
-    hid[...] = hidden
-    out[...] = dot(hidden, wd[...], NT).astype(BF16)
-    hg = dot(u[...], wd[...])
-    gate_grad = (hg * up * s * (1.0 + gate * (1.0 - s))).astype(BF16)
-    up_grad = (hg * gate * s).astype(BF16)
-    gg[...] = gate_grad
-    ug[...] = up_grad
-    rg[...] = (dot(gate_grad, wg[...], NT) + dot(up_grad, wu[...], NT)).astype(BF16)
-
-
-def expert_rows(x, u, wg, wu, wd):
+ORDER_Y = sum((step // SIDE) << (2 * n) for n, step in enumerate(PLANE_STEPS))
+ORDER_X = sum((step % SIDE) << (2 * n) for n, step in enumerate(PLANE_STEPS))
+ORDER_COLUMN = sum(step << (3 * n) for n, step in enumerate(COLUMN_STEPS))
+GROUP = 2
+ROWS = DP * CAP
+SLAB = 256
+
+
+def ordered_plane(n):
+    me = lax.axis_index("expert")
+    y, x = me // SIDE, me % SIDE
+    dy, dx = (ORDER_Y >> (2 * n)) & 3, (ORDER_X >> (2 * n)) & 3
+    ahead = ((y + dy) % SIDE) * SIDE + (x + dx) % SIDE
+    behind = ((y + SIDE - dy) % SIDE) * SIDE + (x + SIDE - dx) % SIDE
+    return ahead, behind
+
+
+def ordered_column(n):
+    me = lax.axis_index("dp")
+    z, core = me // 2, me % 2
+    step = (ORDER_COLUMN >> (3 * n)) & 7
+    dz, other = step // 2, (core + step % 2) % 2
+    return ((z + dz) % SIDE) * 2 + other, ((z + SIDE - dz) % SIDE) * 2 + other
+
+
+def expert_kernel(
+    x, u, wg, wu, wd, out_back, rg_back, dg, du, dd,
+    wgv, wuv, wdv, hid, gg, ug, rows_in, slabs, out_v, rg_v,
+    psend, precv, csend, crecv, wload, rload, sload,
+):
+    dp, ep = lax.axis_index("dp"), lax.axis_index("expert")
+    weights = [
+        pltpu.make_async_copy(src, dst, wload.at[i])
+        for i, (src, dst) in enumerate(((wg, wgv), (wu, wuv), (wd, wdv)))
+    ]
+
+    def row_loads(n, slot):
+        loads = []
+        for part in range(GROUP):
+            source = ordered_plane(n * GROUP + part)[0]
+            for i, src in enumerate((x, u)):
+                loads.append(pltpu.make_async_copy(
+                    src.at[pl.ds(pl.multiple_of(source * ROWS, ROWS), ROWS)],
+                    rows_in.at[i, slot, pl.ds(part * ROWS, ROWS)],
+                    rload.at[i, slot, part],
+                ))
+        return loads
+
+    def slab_loads(n, slot):
+        column = pl.multiple_of(ordered_column(n)[0] * SLAB, SLAB)
+        return [
+            pltpu.make_async_copy(src.at[:, pl.ds(column, SLAB)], slabs.at[i, slot], sload.at[i, slot])
+            for i, src in enumerate((x, u))
+        ]
+
+    def returns(n):
+        target = ordered_plane(n)[0]
+        return [
+            pltpu.make_async_remote_copy(
+                src_ref=src.at[target], dst_ref=dst.at[:, ep],
+                send_sem=psend.at[i, n], recv_sem=precv.at[i, n],
+                device_id=(dp, target), device_id_type=MESH,
+            )
+            for i, (src, dst) in enumerate(((out_v, out_back), (rg_v, rg_back)))
+        ]
+
+    def own_returns():
+        return [
+            pltpu.make_async_copy(src.at[ep], dst.at[:, ep], psend.at[i, EP - 1])
+            for i, (src, dst) in enumerate(((out_v, out_back), (rg_v, rg_back)))
+        ]
+
+    def slices():
+        return ((wgv, dg), (wuv, du), (wdv, dd))
+
+    def grads(n):
+        target = ordered_column(n)[0]
+        part = pl.ds(pl.multiple_of(target * SLAB, SLAB), SLAB)
+        return [
+            pltpu.make_async_remote_copy(
+                src_ref=src.at[part], dst_ref=dst.at[dp],
+                send_sem=csend.at[i, n], recv_sem=crecv.at[i, n],
+                device_id=(target, ep), device_id_type=MESH,
+            )
+            for i, (src, dst) in enumerate(slices())
+        ]
+
+    def own_grads():
+        part = pl.ds(pl.multiple_of(dp * SLAB, SLAB), SLAB)
+        return [
+            pltpu.make_async_copy(src.at[part], dst.at[dp], csend.at[i, DP - 1])
+            for i, (src, dst) in enumerate(slices())
+        ]
+
+    for copy in weights + row_loads(0, 0):
+        copy.start()
+    greet(COLUMN_STEPS, PLANE_STEPS)
+    for copy in weights:
+        copy.wait()
+
+    groups = EP // GROUP
+
+    @pl.loop(0, groups)
+    def _(n):
+        slot = n % 2
+        for copy in row_loads(n, slot):
+            copy.wait()
+
+        @pl.when(n + 1 < groups)
+        def _():
+            for copy in row_loads(n + 1, 1 - slot):
+                copy.start()
+
+        xb, ub = rows_in[0, slot], rows_in[1, slot]
+        gate, up = dot(xb, wgv[...]), dot(xb, wuv[...])
+        s = jax.nn.sigmoid(gate)
+        hidden = (gate * s * up).astype(BF16)
+        out = dot(hidden, wdv[...], NT).astype(BF16)
+        hg = dot(ub, wdv[...])
+        gate_grad = (hg * up * s * (1.0 + gate * (1.0 - s))).astype(BF16)
+        up_grad = (hg * gate * s).astype(BF16)
+        rg = (dot(gate_grad, wgv[...], NT) + dot(up_grad, wuv[...], NT)).astype(BF16)
+        for part in range(GROUP):
+            source = ordered_plane(n * GROUP + part)[0]
+            these = slice(part * ROWS, (part + 1) * ROWS)
+            out_v[source] = out[these].reshape(DP, CAP, -1)
+            rg_v[source] = rg[these].reshape(DP, CAP, -1)
+            held = pl.ds(pl.multiple_of(source * ROWS, ROWS), ROWS)
+            hid[held], gg[held], ug[held] = hidden[these], gate_grad[these], up_grad[these]
+        for part in range(GROUP - 1):
+            for copy in returns(n * GROUP + part):
+                copy.start()
+
+        @pl.when(n + 1 < groups)
+        def _():
+            for copy in returns(n * GROUP + GROUP - 1):
+                copy.start()
+
+        @pl.when(n + 1 == groups)
+        def _():
+            for copy in own_returns() + slab_loads(0, 0):
+                copy.start()
+
+    @pl.loop(0, DP)
+    def _(n):
+        slot = n % 2
+        for copy in slab_loads(n, slot):
+            copy.wait()
+
+        @pl.when(n + 1 < DP)
+        def _():
+            for copy in slab_loads(n + 1, 1 - slot):
+                copy.start()
+
+        part = pl.ds(pl.multiple_of(ordered_column(n)[0] * SLAB, SLAB), SLAB)
+        wgv[part] = dot(slabs[0, slot], gg[...], TN).astype(BF16)
+        wuv[part] = dot(slabs[0, slot], ug[...], TN).astype(BF16)
+        wdv[part] = dot(slabs[1, slot], hid[...], TN).astype(BF16)
+
+        @pl.when(n + 1 < DP)
+        def _():
+            for copy in grads(n):
+                copy.start()
+
+        @pl.when(n + 1 == DP)
+        def _():
+            for copy in own_grads():
+                copy.start()
+
+    for copy in own_returns() + own_grads():
+        copy.wait()
+
+    @pl.loop(0, DP - 1)
+    def _(n):
+        for copy in grads(n):
+            copy.wait()
+
+    @pl.loop(0, EP - 1)
+    def _(n):
+        for copy in returns(n):
+            copy.wait()
+
+
+def expert(x, u, wg, wu, wd):
     rows, width = x.shape
     ff = wg.shape[1]
-    block = 256
-    wide = pl.BlockSpec((block, width), lambda i: (i, 0))
-    thin = pl.BlockSpec((block, ff), lambda i: (i, 0))
-    weight = pl.BlockSpec((width, ff), lambda i: (0, 0), pipeline_mode=pl.Buffered(1))
+    dma = pltpu.SemaphoreType.DMA
     return pl.pallas_call(
-        rows_kernel,
-        grid=(rows // block,),
-        out_shape=[jax.ShapeDtypeStruct((rows, width), BF16)] * 2
-        + [jax.ShapeDtypeStruct((rows, ff), BF16)] * 3,
-        in_specs=[wide, wide, weight, weight, weight],
-        out_specs=[wide, wide, thin, thin, thin],
-        compiler_params=pltpu.CompilerParams(vmem_limit_bytes=56 * 2**20),
-        name="expert_rows",
+        expert_kernel,
+        out_shape=[jax.ShapeDtypeStruct((DP, EP, CAP, width), BF16)] * 2
+        + [jax.ShapeDtypeStruct((DP, width // DP, ff), BF16)] * 3,
+        in_specs=[ANY] * 5,
+        out_specs=[ANY] * 5,
+        scratch_shapes=[pltpu.VMEM((width, ff), BF16)] * 3
+        + [pltpu.VMEM((rows, ff), BF16)] * 3
+        + [
+            pltpu.VMEM((2, 2, GROUP * ROWS, width), BF16),
+            pltpu.VMEM((2, 2, rows, SLAB), BF16),
+            pltpu.VMEM((EP, DP, CAP, width), BF16),
+            pltpu.VMEM((EP, DP, CAP, width), BF16),
+            dma((2, EP)), dma((2, EP)), dma((3, DP)), dma((3, DP)),
+            dma((3,)), dma((2, 2, GROUP)), dma((2, 2)),
+        ],
+        compiler_params=pltpu.CompilerParams(
+            collective_id=2, has_side_effects=True, vmem_limit_bytes=62 * 2**20
+        ),
+        name="expert",
     )(x, u, wg, wu, wd)
-
-
-def weights_kernel(x, u, hid, gg, ug, dg, du, dd):
-    dg[...] = dot(x[...], gg[...], TN).astype(BF16)
-    du[...] = dot(x[...], ug[...], TN).astype(BF16)
-    dd[...] = dot(u[...], hid[...], TN).astype(BF16)
-
-
-def expert_weights(x, u, hid, gg, ug):
-    rows, width = x.shape
-    ff = hid.shape[1]
-    block = 256
-    slab = pl.BlockSpec((rows, block), lambda i: (0, i))
-    whole = pl.BlockSpec((rows, ff), lambda i: (0, 0), pipeline_mode=pl.Buffered(1))
-    result = pl.BlockSpec((block, ff), lambda i: (i, 0))
-    return pl.pallas_call(
-        weights_kernel,
-        grid=(width // block,),
-        out_shape=[jax.ShapeDtypeStruct((width, ff), BF16)] * 3,
-        in_specs=[slab, slab, whole, whole, whole],
-        out_specs=[result] * 3,
-        compiler_params=pltpu.CompilerParams(vmem_limit_bytes=56 * 2**20),
-        name="expert_weights",
-    )(x, u, hid, gg, ug)
 
 
 def local(tokens, expert_ids, gate_codes, grad_out, w_gate, w_up, w_down):
@@ -322,16 +461,11 @@
         return summed.astype(BF16)
 
     x, u, wg, wu, wd = exchange(
-        True, 1, spread(pick, tok_all), spread(weight, grd_all), w_gate, w_up, w_down
+        spread(pick, tok_all), spread(weight, grd_all), w_gate, w_up, w_down
     )
     x, u = x.reshape(-1, width), u.reshape(-1, width)
     wg, wu, wd = (w.reshape(width, ff) for w in (wg, wu, wd))
-    out, rg, hid, gg, ug = expert_rows(x, u, wg, wu, wd)
-    grads = expert_weights(x, u, hid, gg, ug)
-    shape = (EP, DP, CAP, width)
-    out, rg, dg, du, dd = exchange(
-        False, 2, out.reshape(shape), rg.reshape(shape), *(g.reshape(DP, -1, ff) for g in grads)
-    )
+    out, rg, dg, du, dd = expert(x, u, wg, wu, wd)
     mixed, tokens_grad = scatter_column(collect(weight, out), collect(pick, rg))
     mixed, tokens_grad = (
         jnp.sum(v.astype(F32), axis=0).astype(BF16) for v in (mixed, tokens_grad)

time: 685 us -> 595 us (0.87)
  Pallas kernels: 643 us -> 556 us
    pallas_call x4 -> x2, Pallas kernels: 532 us -> 447 us  [the longest x1 230 us: exchange(): pl.pallas_call(exchange_kernel, out_shape=[jax.ShapeDtypeStruct((EP, DP,...]
where the time goes in v2:
time: 595 us
  Pallas kernels  556 us (93%)
  matrix products  19.8 us (3%)
  local copies, waits for them, and re-layouts  11 us (2%)
  other arithmetic  7.2 us (1%)
    pallas_call x1, Pallas kernels, exchange(): pl.pallas_call(exchange_kernel, out_shape=[jax.ShapeDtypeStruct((EP, DP,...  230 us
    pallas_call x1, Pallas kernels, expert(): pl.pallas_call(expert_kernel, out_shape=[jax.ShapeDtypeStruct((DP, EP, CA...  217 us
    pallas_call x1, Pallas kernels, gather_column(): pl.pallas_call(gather_kernel, out_shape=[jax.ShapeDtypeStruct((DP,) + tok...  55.3 us
    pallas_call x1, Pallas kernels, scatter_column(): pl.pallas_call(scatter_kernel, out_shape=[jax.ShapeDtypeStruct((SIDE, tok...  54.2 us
    dot_general x2, matrix products, spread(): picked = lax.dot_general(matrix, rows, gathers, preferred_element_type=F32)  13.4 us

profile of v2, /device:TPU:3, one launch (start us, length us, event | category | flops | bytes accessed | tf_op | source)
XLA Modules:
  0.0 595.2 jit_solution(2886935732750462145)
XLA Ops:
  0.6 1.3 add_bitcast_fusion.meta
  2.0 0.1 eq.42
  2.0 55.3 %gather_column.1 = (bf16[8,128,2048]{2,1,0:T(8,128)(2,1)}, bf16[8,128,2048]{2,1,0:T(8,128)(2,1)}, s32[8,8,128]{2,1,0:T(8,128)}) custom-call(bf16[128,2048]{1,0:T(8,128)(2,1)} %tok.1, bf16[128,2048]{1,0:T(8,128)(2,1)} %grd.1, s32[8,128]{1,0:T(8,128)} %add_bitcast_fusion.meta), custom_call_target="tpu_custom_call" | custom-call | tf_op jit(solution)/shard_map/gather_column/pallas_call | solution.py:101
  57.3 0.8 add_select_fusion.1
  58.1 0.2 compare_reduce_fusion
  58.3 0.2 fusion.2
  58.6 0.1 fusion
  58.7 0.2 bitcast_compare_fusion
  59.0 0.2 fusion.1
  59.2 0.0 copy-start.1
  59.2 7.9 %convolution_convert_fusion = bf16[8,256,2048]{2,1,0:T(8,128)(2,1)} fusion(bf16[8,256,128]{2,1,0:T(8,128)(2,1)S(1)} %fusion.1, bf16[8,128,2048]{2,1,0:T(8,128)(2,1)} %get-tuple-element.22), kind=kOutput, calls=%fused_computation | convolution fusion | flops 1077936128 | bytes 13107200 | tf_op jit(solution)/shard_map/dot_general | solution.py:454
  67.1 0.0 copy-done.1
  67.1 5.5 convolution_convert_fusion.1
  72.6 229.8 %exchange.1 = (bf16[16,8,16,2048]{3,2,1,0:T(8,128)(2,1)}, bf16[16,8,16,2048]{3,2,1,0:T(8,128)(2,1)}, bf16[8,256,768]{2,1,0:T(8,128)(2,1)}, bf16[8,256,768]{2,1,0:T(8,128)(2,1)}, bf16[8,256,768]{2,1,0:T(8,128)(2,1)}) custom-call(bf16[8,16,16,2048]{3,2,1,0:T(8,128)(2,1)} %bitcast.36, bf16[8,16,16,2048]{3,2,1,0:T(8,128)(2,1)} %bitcast.35, ...), custom_call_target="tpu_custom_call" | custom-call | tf_op jit(solution)/shard_map/exchange/pallas_call | solution.py:148
  302.4 217.1 %expert.1 = (bf16[8,16,16,2048]{3,2,1,0:T(8,128)(2,1)}, bf16[8,16,16,2048]{3,2,1,0:T(8,128)(2,1)}, bf16[8,256,768]{2,1,0:T(8,128)(2,1)}, bf16[8,256,768]{2,1,0:T(8,128)(2,1)}, bf16[8,256,768]{2,1,0:T(8,128)(2,1)}) custom-call(bf16[2048,2048]{1,0:T(8,128)(2,1)} %bitcast.41, bf16[2048,2048]{1,0:T(8,128)(2,1)} %bitcast.42, bf16[2048,768]{1,0:T(8,128)(2,1)} %bitcast.43, ...), custom_call_target="tpu_custom_call" | custom-call | tf_op jit(solution)/shard_map/expert/pallas_call | solution.py:410
  519.6 0.0 slice-start
  519.6 0.0 slice-start.1
  519.6 4.9 convolution_convert_fusion.3
  524.4 0.0 slice-done
  524.5 1.0 slice-done.1
  525.4 1.3 convolution_convert_fusion.2
  526.8 54.2 %scatter_column.1 = (bf16[4,128,2048]{2,1,0:T(8,128)(2,1)S(1)}, bf16[4,128,2048]{2,1,0:T(8,128)(2,1)S(1)}) custom-call(bf16[4,2,128,2048]{3,2,1,0:T(8,128)(2,1)S(1)} %bitcast.33, bf16[4,2,128,2048]{3,2,1,0:T(8,128)(2,1)S(1)} %bitcast.34), custom_call_target="tpu_custom_call" | custom-call | tf_op jit(solution)/shard_map/scatter_column/pallas_call | solution.py:195
  581.0 0.0 copy-start
  581.0 1.3 copy-done
  582.3 2.9 reduce_sum.34
  585.2 1.3 reduce_sum.35
  586.6 0.0 copy-start.3
  586.6 3.9 copy.27
  590.5 0.0 copy-done.3
  590.5 0.0 copy-start.2
  590.5 1.7 copy.28
  592.1 1.4 copy-done.2
  593.5 1.7 copy.29
  (4 shorter events, 0.0 us)
Async XLA Ops:
  59.2 7.9 %copy-start.1 = (bf16[8,128,2048]{2,1,0:T(8,128)(2,1)S(1)}, bf16[8,128,2048]{2,1,0:T(8,128)(2,1)}, u32[]{:S(2)}) copy-start(bf16[8,128,2048]{2,1,0:T(8,128)(2,1)} %get-tuple-element.21) | copy-start | bytes 12582916
  519.6 4.9 slice-start
  519.6 5.8 slice-start.1
  581.0 1.3 copy-start
  586.6 3.9 copy-start.3
  590.5 3.0 copy-start.2

commit v3 on v2

v3 whole, which is shorter than its diff:
```python
import jax
import jax.numpy as jnp
from jax import lax
from jax.experimental import pallas as pl
from jax.experimental.pallas import tpu as pltpu
from jax.sharding import PartitionSpec as P

BF16 = jnp.bfloat16
F32 = jnp.float32
MESH = pl.DeviceIdType.MESH
ANY = pl.BlockSpec(memory_space=pl.ANY)
VMEM = pl.BlockSpec(memory_space=pltpu.VMEM)
DP = 8
EP = 16
SIDE = 4
CAP = 16
TOK = 128


def column_peer(step):
    me = lax.axis_index("dp")
    z, core = me // 2, me % 2
    dz, other = step // 2, (core + step % 2) % 2
    return ((z + dz) % SIDE) * 2 + other, ((z + SIDE - dz) % SIDE) * 2 + other


def plane_peer(step):
    me = lax.axis_index("expert")
    y, x = me // SIDE, me % SIDE
    dy, dx = step // SIDE, step % SIDE
    ahead = ((y + dy) % SIDE) * SIDE + (x + dx) % SIDE
    behind = ((y + SIDE - dy) % SIDE) * SIDE + (x + SIDE - dx) % SIDE
    return ahead, behind


PLANE_STEPS = (1, 3, 4, 12, 5, 15, 7, 13, 10, 2, 8, 6, 14, 9, 11)
COLUMN_STEPS = (4, 5, 2, 3, 6, 7, 1)


def greet(column, plane):
    barrier = pltpu.get_barrier_semaphore()
    dp, ep = lax.axis_index("dp"), lax.axis_index("expert")
    count = 0
    for step in column:
        pl.semaphore_signal(barrier, inc=1, device_id=(column_peer(step)[0], ep), device_id_type=MESH)
        count += 1
    for step in plane:
        pl.semaphore_signal(barrier, inc=1, device_id=(dp, plane_peer(step)[0]), device_id_type=MESH)
        count += 1
    pl.semaphore_wait(barrier, count)


def to_column(step, src, dst, send, recv):
    return pltpu.make_async_remote_copy(
        src_ref=src, dst_ref=dst, send_sem=send, recv_sem=recv,
        device_id=(column_peer(step)[0], lax.axis_index("expert")), device_id_type=MESH,
    )


def to_plane(step, src, dst, send, recv):
    return pltpu.make_async_remote_copy(
        src_ref=src, dst_ref=dst, send_sem=send, recv_sem=recv,
        device_id=(lax.axis_index("dp"), plane_peer(step)[0]), device_id_type=MESH,
    )


def gather_kernel(tok, meta, tok_all, meta_all, send, recv, fsend, frecv, local):
    me = lax.axis_index("dp")
    greet((2, 4, 6, 1), ())
    pairs = ((meta, meta_all), (tok, tok_all))
    copies = []
    for i, (src, dst) in enumerate(pairs):
        for n, step in enumerate((4, 2, 6, 1)):
            copy = to_column(step, src, dst.at[me], send.at[i, n], recv.at[i, n])
            copy.start()
            copies.append(copy)
    locals_ = []
    for i, (src, dst) in enumerate(pairs):
        copy = pltpu.make_async_copy(src, dst.at[me], local.at[i])
        copy.start()
        locals_.append(copy)
    forwards = []
    for i, (src, dst) in enumerate(pairs):
        for n, step in ((1, 2), (2, 6), (0, 4)):
            behind = column_peer(step)[1]
            copies[4 * i + n].wait_recv()
            copy = to_column(1, dst.at[behind], dst.at[behind], fsend.at[i, n], frecv.at[i, n])
            copy.start()
            forwards.append(copy)
    for i in range(2):
        copies[4 * i + 3].wait_recv()
    for copy in copies:
        copy.wait_send()
    for copy in forwards:
        copy.wait()
    for copy in locals_:
        copy.wait()


def gather_column(tok, meta):
    dma = pltpu.SemaphoreType.DMA
    return pl.pallas_call(
        gather_kernel,
        out_shape=[
            jax.ShapeDtypeStruct((DP,) + tok.shape, tok.dtype),
            jax.ShapeDtypeStruct((DP,) + meta.shape, meta.dtype),
        ],
        in_specs=[ANY] * 2,
        out_specs=[ANY] * 2,
        scratch_shapes=[dma((2, 4)), dma((2, 4)), dma((2, 3)), dma((2, 3)), dma((2,))],
        compiler_params=pltpu.CompilerParams(collective_id=0, has_side_effects=True),
        name="gather_column",
    )(tok, meta)


PEERS = EP - 1
SENDS = DP * PEERS
WINDOW = 24
HALF = DP // 2


def exchange_kernel(tok_all, grd, pick, weight, p, q, r, a_out, b_out, p_out, q_out, r_out,
                    grd_all, tok_rows, grd_rows,
                    psend, precv, csend, crecv, gsend, grecv, fsend, frecv, local):
    dp, ep = lax.axis_index("dp"), lax.axis_index("expert")
    greet(COLUMN_STEPS, PLANE_STEPS)
    gathers = [
        to_column(step, grd, grd_all.at[dp], gsend.at[n], grecv.at[n]) for n, step in enumerate((4, 2, 6, 1))
    ]
    own = pltpu.make_async_copy(grd, grd_all.at[dp], local.at[5])
    columns = []
    for n, step in enumerate(COLUMN_STEPS):
        target = column_peer(step)[0]
        for i, (src, dst) in enumerate(((p, p_out), (q, q_out), (r, r_out))):
            columns.append(to_column(step, src.at[target], dst.at[dp], csend.at[i, n], crecv.at[i, n]))
    for i, (src, dst) in enumerate(((p, p_out), (q, q_out), (r, r_out))):
        columns.append(pltpu.make_async_copy(src.at[dp], dst.at[dp], local.at[i]))
    own_rows = [
        pltpu.make_async_copy(src.at[ep], dst.at[ep], local.at[3 + i])
        for i, (src, dst) in enumerate(((tok_rows, a_out), (grd_rows, b_out)))
    ]
    ends = ((tok_rows, a_out), (grd_rows, b_out))

    def plane(i, k):
        src, dst = ends[i]
        target, part = ordered_plane(k % PEERS)[0], k // PEERS
        return pltpu.make_async_remote_copy(
            src_ref=src.at[target, part], dst_ref=dst.at[ep, part],
            send_sem=psend.at[i, k], recv_sem=precv.at[i, k],
            device_id=(dp, target), device_id_type=MESH,
        )

    def go_on(i, start, stop):
        @pl.loop(start, stop)
        def _(k):
            plane(i, k - WINDOW).wait_send()
            plane(i, k).start()

    def spread(matrix, rows, result, start, stop):
        @pl.loop(start, stop)
        def _(source):
            picked = dot(matrix[source], rows[source]).astype(BF16)
            result[:, source] = picked.reshape(EP, CAP, picked.shape[-1])

    for copy in gathers + [own]:
        copy.start()
    spread(pick, tok_all, tok_rows, 0, HALF)

    @pl.loop(0, WINDOW)
    def _(k):
        plane(0, k).start()

    spread(pick, tok_all, tok_rows, HALF, DP)
    own_rows[0].start()
    go_on(0, WINDOW, 56)
    forwards = []
    for n, step in ((1, 2), (2, 6), (0, 4)):
        behind = column_peer(step)[1]
        gathers[n].wait_recv()
        copy = to_column(1, grd_all.at[behind], grd_all.at[behind], fsend.at[n], frecv.at[n])
        copy.start()
        forwards.append(copy)
    for copy in columns:
        copy.start()
    go_on(0, 56, 100)
    gathers[3].wait_recv()
    for copy in forwards:
        copy.wait_recv()
    own.wait()
    spread(weight, grd_all, grd_rows, 0, DP)
    own_rows[1].start()
    go_on(0, 100, SENDS)

    @pl.loop(0, WINDOW)
    def _(k):
        plane(0, SENDS - WINDOW + k).wait_send()
        plane(1, k).start()

    go_on(1, WINDOW, SENDS)

    @pl.loop(SENDS - WINDOW, SENDS)
    def _(k):
        plane(1, k).wait_send()

    for i in range(2):

        @pl.loop(0, SENDS)
        def _(k):
            plane(i, k).wait_recv()

    for copy in gathers + forwards:
        copy.wait_send()
    for copy in columns + own_rows:
        copy.wait()


def exchange(tok_all, grd, pick, weight, p, q, r):
    tok, width = grd.shape
    dma = pltpu.SemaphoreType.DMA
    rows = (EP, DP, CAP, width)
    return pl.pallas_call(
        exchange_kernel,
        out_shape=[jax.ShapeDtypeStruct(rows, BF16)] * 2 + [jax.ShapeDtypeStruct(p.shape, BF16)] * 3,
        in_specs=[VMEM, ANY, VMEM, VMEM, ANY, ANY, ANY],
        out_specs=[ANY] * 5,
        scratch_shapes=[
            pltpu.VMEM((DP, tok, width), BF16),
            pltpu.VMEM(rows, BF16),
            pltpu.VMEM(rows, BF16),
            dma((2, SENDS)), dma((2, SENDS)), dma((3, DP - 1)), dma((3, DP - 1)),
            dma((4,)), dma((4,)), dma((3,)), dma((3,)), dma((6,)),
        ],
        compiler_params=pltpu.CompilerParams(
            collective_id=1, has_side_effects=True, vmem_limit_bytes=63 * 2**20
        ),
        name="exchange",
    )(tok_all, grd, pick, weight, p, q, r)


NT = (((1,), (1,)), ((), ()))
TN = (((0,), (0,)), ((), ()))


def dot(a, b, dims=(((1,), (0,)), ((), ()))):
    return lax.dot_general(a, b, dims, preferred_element_type=F32)


ORDER_Y = sum((step // SIDE) << (2 * n) for n, step in enumerate(PLANE_STEPS))
ORDER_X = sum((step % SIDE) << (2 * n) for n, step in enumerate(PLANE_STEPS))
ORDER_COLUMN = sum(step << (3 * n) for n, step in enumerate(COLUMN_STEPS))
GROUP = 2
ROWS = DP * CAP
SLAB = 256


def ordered_plane(n):
    me = lax.axis_index("expert")
    y, x = me // SIDE, me % SIDE
    dy, dx = (ORDER_Y >> (2 * n)) & 3, (ORDER_X >> (2 * n)) & 3
    ahead = ((y + dy) % SIDE) * SIDE + (x + dx) % SIDE
    behind = ((y + SIDE - dy) % SIDE) * SIDE + (x + SIDE - dx) % SIDE
    return ahead, behind


def ordered_column(n):
    me = lax.axis_index("dp")
    z, core = me // 2, me % 2
    step = (ORDER_COLUMN >> (3 * n)) & 7
    dz, other = step // 2, (core + step % 2) % 2
    return ((z + dz) % SIDE) * 2 + other, ((z + SIDE - dz) % SIDE) * 2 + other


def expert_kernel(
    x, u, wg, wu, wd, weight, pick, mixed, tokens_grad, out_back, rg_back, dg, du, dd,
    wgv, wuv, wdv, hid, gg, ug, rows_in, slabs, out_v, rg_v, paired, arrived,
    psend, precv, csend, crecv, wload, rload, sload, own, bload, xsend, xrecv, zsend, zrecv,
):
    dp, ep = lax.axis_index("dp"), lax.axis_index("expert")
    z, core = dp // 2, dp % 2
    weights = [
        pltpu.make_async_copy(src, dst, wload.at[i])
        for i, (src, dst) in enumerate(((wg, wgv), (wu, wuv), (wd, wdv)))
    ]
    backs = ((out_v, out_back), (rg_v, rg_back))

    def ahead(n):
        return (0b00110110 >> (2 * n)) & 3

    def row_loads(n, slot):
        loads = []
        for part in range(GROUP):
            source = ordered_plane(n * GROUP + part)[0]
            for i, src in enumerate((x, u)):
                loads.append(pltpu.make_async_copy(
                    src.at[source], rows_in.at[i, slot, pl.ds(part * DP, DP)], rload.at[i, slot, part]
                ))
        return loads

    def slab_loads(n, slot):
        column = pl.multiple_of(ordered_column(n)[0] * SLAB, SLAB)
        return [
            pltpu.make_async_copy(src.at[:, :, :, pl.ds(column, SLAB)], slabs.at[i, slot], sload.at[i, slot])
            for i, src in enumerate((x, u))
        ]

    def back(i, k):
        src, dst = backs[i]
        n, part = (k // DP, k % DP) if i == 0 else (k % PEERS, k // PEERS)
        target = ordered_plane(n)[0]
        part = (z + ahead(part // 2)) % SIDE * 2 + part % 2
        return pltpu.make_async_remote_copy(
            src_ref=src.at[target, part], dst_ref=dst.at[ep, part],
            send_sem=psend.at[i, k], recv_sem=precv.at[i, k],
            device_id=(dp, target), device_id_type=MESH,
        )

    def own_back(i):
        return pltpu.make_async_copy(backs[i][0].at[ep], backs[i][1].at[ep], own.at[i])

    slices = ((wgv, dg), (wuv, du), (wdv, dd))

    def grads(n):
        target = ordered_column(n)[0]
        part = pl.ds(pl.multiple_of(target * SLAB, SLAB), SLAB)
        return [
            pltpu.make_async_remote_copy(
                src_ref=src.at[part], dst_ref=dst.at[dp],
                send_sem=csend.at[i, n], recv_sem=crecv.at[i, n],
                device_id=(target, ep), device_id_type=MESH,
            )
            for i, (src, dst) in enumerate(slices)
        ]

    def own_grads():
        part = pl.ds(pl.multiple_of(dp * SLAB, SLAB), SLAB)
        return [
            pltpu.make_async_copy(src.at[part], dst.at[dp], own.at[2 + i])
            for i, (src, dst) in enumerate(slices)
        ]

    def back_load(i, source, slot):
        return pltpu.make_async_copy(backs[i][1].at[:, source], rows_in.at[0, slot], bload.at[slot])

    def pair_copy(i, n):
        place = ((z + ahead(n)) % SIDE) * 2 + 1 - core
        return to_column(1, out_v.at[place], paired.at[i, n], xsend.at[i, n], xrecv.at[i, n])

    def z_copy(i, n):
        place = ((z + ahead(n)) % SIDE) * 2 + core
        return to_column(2 * ahead(n), out_v.at[place], arrived.at[i, n], zsend.at[i, n], zrecv.at[i, n])

    def collect(i, matrix, n):
        chip = (z + ahead(n)) % SIDE
        places = (chip * 2 + 1 - core, chip * 2 + core)
        for slot in range(2):
            back_load(i, places[slot], slot).start()
        for slot in range(2):
            back_load(i, places[slot], slot).wait()
            held = rows_in[0, slot]
            summed = dot(matrix[places[slot]], held.reshape(EP * CAP, held.shape[-1]), TN).astype(BF16)
            out_v[places[slot]] = summed.reshape(out_v.shape[1:])
            if slot == 0:
                pair_copy(i, n).start()

    def add_pair(i, n):
        place = ((z + ahead(n)) % SIDE) * 2 + core
        pair_copy(i, n).wait_recv()
        out_v[place] = (out_v[place].astype(F32) + paired[i, n].astype(F32)).astype(BF16)
        if n < SIDE - 1:
            z_copy(i, n).start()

    def finish(i, result):
        total = out_v[dp].astype(F32)
        for n in range(SIDE - 1):
            z_copy(i, n).wait_recv()
            total += arrived[i, n].astype(F32)
        result[...] = total.astype(BF16).reshape(result.shape)
        for n in range(SIDE):
            pair_copy(i, n).wait_send()
        for n in range(SIDE - 1):
            z_copy(i, n).wait_send()

    for copy in weights + row_loads(0, 0):
        copy.start()
    greet(COLUMN_STEPS, PLANE_STEPS)
    for copy in weights:
        copy.wait()

    groups = EP // GROUP

    @pl.loop(0, groups)
    def _(n):
        slot = n % 2
        for copy in row_loads(n, slot):
            copy.wait()

        @pl.when(n + 1 < groups)
        def _():
            for copy in row_loads(n + 1, 1 - slot):
                copy.start()

        shape = (GROUP * ROWS, rows_in.shape[-1])
        xb, ub = rows_in[0, slot].reshape(shape), rows_in[1, slot].reshape(shape)
        gate, up = dot(xb, wgv[...]), dot(xb, wuv[...])
        s = jax.nn.sigmoid(gate)
        hidden = (gate * s * up).astype(BF16)
        out = dot(hidden, wdv[...], NT).astype(BF16)
        hg = dot(ub, wdv[...])
        gate_grad = (hg * up * s * (1.0 + gate * (1.0 - s))).astype(BF16)
        up_grad = (hg * gate * s).astype(BF16)
        rg = (dot(gate_grad, wgv[...], NT) + dot(up_grad, wuv[...], NT)).astype(BF16)
        for part in range(GROUP):
            source = ordered_plane(n * GROUP + part)[0]
            these = slice(part * ROWS, (part + 1) * ROWS)
            out_v[source] = out[these].reshape(DP, CAP, -1)
            rg_v[source] = rg[these].reshape(DP, CAP, -1)
            held = pl.ds(pl.multiple_of(source * ROWS, ROWS), ROWS)
            hid[held], gg[held], ug[held] = hidden[these], gate_grad[these], up_grad[these]
        @pl.loop(0, 12)
        def _(j):
            back(0, n * 12 + j).start()

    first = 12 * groups

    for i in range(2):
        own_back(i).start()
    for copy in slab_loads(0, 0):
        copy.start()

    @pl.loop(0, DP)
    def _(n):
        slot = n % 2
        for copy in slab_loads(n, slot):
            copy.wait()

        @pl.when(n + 1 < DP)
        def _():
            for copy in slab_loads(n + 1, 1 - slot):
                copy.start()

        part = pl.ds(pl.multiple_of(ordered_column(n)[0] * SLAB, SLAB), SLAB)
        shape = (EP * ROWS, SLAB)
        wgv[part] = dot(slabs[0, slot].reshape(shape), gg[...], TN).astype(BF16)
        wuv[part] = dot(slabs[0, slot].reshape(shape), ug[...], TN).astype(BF16)
        wdv[part] = dot(slabs[1, slot].reshape(shape), hid[...], TN).astype(BF16)

        @pl.when(n + 1 < DP)
        def _():
            for copy in grads(n):
                copy.start()

        @pl.when(n + 1 == DP)
        def _():
            for copy in own_grads():
                copy.start()

        @pl.when(n < (SENDS - first) // 4)
        def _():
            for j in range(4):
                back(0, first - WINDOW + 4 * n + j).wait_send()
                back(0, first + 4 * n + j).start()

    @pl.loop(0, WINDOW)
    def _(k):
        back(0, SENDS - WINDOW + k).wait_send()
        back(1, k).start()

    def go_on(start, stop):
        @pl.loop(start, stop)
        def _(k):
            back(1, k - WINDOW).wait_send()
            back(1, k).start()

    go_on(WINDOW, 56)

    @pl.loop(0, first - WINDOW)
    def _(k):
        back(0, k).wait_send()

    @pl.loop(0, SENDS)
    def _(k):
        back(0, k).wait_recv()

    own_back(0).wait()
    for n in range(SIDE):
        collect(0, weight, n)
    go_on(56, 80)
    for n in range(SIDE):
        add_pair(0, n)
    go_on(80, 104)
    finish(0, mixed)
    go_on(104, SENDS)
    own_back(1).wait()
    for n in range(SIDE):

        @pl.loop(n * 2 * PEERS, (n + 1) * 2 * PEERS)
        def _(k):
            back(1, k).wait_recv()

        collect(1, pick, n)
        if n > 0:
            add_pair(1, n - 1)
    add_pair(1, SIDE - 1)
    finish(1, tokens_grad)

    @pl.loop(SENDS - WINDOW, SENDS)
    def _(k):
        back(1, k).wait_send()

    for copy in own_grads():
        copy.wait()

    @pl.loop(0, DP - 1)
    def _(n):
        for copy in grads(n):
            copy.wait()


def expert(x, u, wg, wu, wd, weight, pick):
    width = x.shape[-1]
    ff = wg.shape[1]
    tok = weight.shape[-1]
    dma = pltpu.SemaphoreType.DMA
    block = (DP, CAP, width)
    results = pl.pallas_call(
        expert_kernel,
        out_shape=[jax.ShapeDtypeStruct((tok, width), BF16)] * 2
        + [jax.ShapeDtypeStruct((EP, DP, CAP, width), BF16)] * 2
        + [jax.ShapeDtypeStruct((DP, width // DP, ff), BF16)] * 3,
        in_specs=[ANY] * 5 + [VMEM] * 2,
        out_specs=[VMEM] * 2 + [ANY] * 5,
        scratch_shapes=[pltpu.VMEM((width, ff), BF16)] * 3
        + [pltpu.VMEM((EP * ROWS, ff), BF16)] * 3
        + [
            pltpu.VMEM((2, 2, GROUP * DP, CAP, width), BF16),
            pltpu.VMEM((2, 2, EP, DP, CAP, SLAB), BF16),
            pltpu.VMEM((EP,) + block, BF16),
            pltpu.VMEM((EP,) + block, BF16),
            pltpu.VMEM((2, SIDE) + block, BF16),
            pltpu.VMEM((2, SIDE - 1) + block, BF16),
            dma((2, SENDS)), dma((2, SENDS)), dma((3, DP - 1)), dma((3, DP - 1)),
            dma((3,)), dma((2, 2, GROUP)), dma((2, 2)), dma((5,)), dma((2,)),
            dma((2, SIDE)), dma((2, SIDE)), dma((2, SIDE - 1)), dma((2, SIDE - 1)),
        ],
        compiler_params=pltpu.CompilerParams(
            collective_id=2, has_side_effects=True, vmem_limit_bytes=63 * 2**20
        ),
        name="expert",
    )(x, u, wg, wu, wd, weight, pick)
    return results[0], results[1], *results[4:]


def local(tokens, expert_ids, gate_codes, grad_out, w_gate, w_up, w_down):
    dp = lax.axis_index("dp")
    tok, width = tokens.shape
    ff = w_gate.shape[-1]
    meta = (expert_ids * 256 + gate_codes).T
    tok_all, meta_all = gather_column(tokens, meta)
    ids, codes = meta_all // 256, meta_all % 256
    mine = jnp.arange(EP, dtype=jnp.int32) * DP + dp
    named = ids[:, None] == mine[None, :, None, None]
    has = jnp.any(named, axis=2)
    gate = jnp.sum(jnp.where(named, codes[:, None], 0), axis=2).astype(F32) / 256.0
    earlier = jnp.triu(jnp.ones((tok, tok), BF16), 1)
    rank = jnp.dot(has.astype(BF16), earlier, preferred_element_type=F32).astype(jnp.int32)
    slot = jnp.where(has, rank, -1)[:, :, None, :]
    pick = slot == jnp.arange(CAP, dtype=jnp.int32)[None, None, :, None]
    weight = jnp.where(pick, gate[:, :, None, :], 0.0).astype(BF16).reshape(DP, EP * CAP, tok)
    pick = pick.astype(BF16).reshape(DP, EP * CAP, tok)
    x, u, wg, wu, wd = exchange(tok_all, grad_out, pick, weight, w_gate, w_up, w_down)
    wg, wu, wd = (w.reshape(width, ff) for w in (wg, wu, wd))
    return expert(x, u, wg, wu, wd, weight, pick)


def solution(mesh):
    rows, weights = P(("dp", "expert"), None), P("expert", "dp", None)
    return jax.shard_map(
        local,
        mesh=mesh,
        in_specs=(rows,) * 4 + (weights,) * 3,
        out_specs=(rows,) * 2 + (weights,) * 3,
        check_vma=False,
    )
```

time: 595 us -> 495 us (0.83); the launches traced: 595 us -> 487 us
  Pallas kernels: 556 us -> 469 us
  matrix products: 19.8 us -> 0.14 us
    pallas_call x3 -> x2, Pallas kernels: 501 us -> 437 us  [the longest x1 240 us: expert(): pl.pallas_call(expert_kernel, out_shape=[jax.ShapeDtypeStruct((tok, width...]
    pallas_call x1, Pallas kernels: 55.3 us -> 32.7 us  [gather_column(): pl.pallas_call(gather_kernel, out_shape=[jax.ShapeDtypeStruct((DP,) + tok...]
    dot_general x4 -> x0, matrix products: 19.6 us -> none  [the longest x2 13.4 us: spread(): picked = lax.dot_general(matrix, rows, gathers, preferred_element_type=F32)]
    unnamed x15 -> x9, local copies, waits for them, and re-layouts: 10.9 us -> 12.4 us
where the time goes in v3:
time: 495 us; the launch traced here: 487 us
  Pallas kernels  469 us (95%)
  local copies, waits for them, and re-layouts  12.4 us (3%)
    pallas_call x1, Pallas kernels, expert(): pl.pallas_call(expert_kernel, out_shape=[jax.ShapeDtypeStruct((tok, width...  240 us
    pallas_call x1, Pallas kernels, exchange(): pl.pallas_call(exchange_kernel, out_shape=[jax.ShapeDtypeStruct(rows, BF1...  197 us
    pallas_call x1, Pallas kernels, gather_column(): pl.pallas_call(gather_kernel, out_shape=[jax.ShapeDtypeStruct((DP,) + tok...  32.7 us
    unnamed x9, local copies, waits for them, and re-layouts  12.4 us

profile of v3, /device:TPU:3, one launch (start us, length us, event | category | flops | bytes accessed | tf_op | source)
XLA Modules:
  0.0 487.3 jit_solution(5090033436294289401)
XLA Ops:
  0.6 1.3 add_bitcast_fusion.meta
  2.0 0.1 eq.42
  2.0 32.7 %gather_column.1 = (bf16[8,128,2048]{2,1,0:T(8,128)(2,1)}, s32[8,8,128]{2,1,0:T(8,128)}) custom-call(bf16[128,2048]{1,0:T(8,128)(2,1)} %tok.1, s32[8,128]{1,0:T(8,128)} %add_bitcast_fusion.meta), custom_call_target="tpu_custom_call" | custom-call | tf_op jit(solution)/shard_map/gather_column/pallas_call | solution.py:102
  34.7 0.8 add_select_fusion
  35.5 0.2 compare_reduce_fusion
  35.7 0.2 fusion.3
  36.0 0.1 fusion
  36.1 1.0 fusion.1.weight
  37.1 1.0 fusion.2.pick
  38.1 196.7 %exchange.1 = (bf16[16,8,16,2048]{3,2,1,0:T(8,128)(2,1)}, bf16[16,8,16,2048]{3,2,1,0:T(8,128)(2,1)}, bf16[8,256,768]{2,1,0:T(8,128)(2,1)}, bf16[8,256,768]{2,1,0:T(8,128)(2,1)}, bf16[8,256,768]{2,1,0:T(8,128)(2,1)}) custom-call(bf16[8,128,2048]{2,1,0:T(8,128)(2,1)} %get-tuple-element.17.tok_all, bf16[128,2048]{1,0:T(8,128)(2,1)} %grd.1, ...), custom_call_target="tpu_custom_call" | custom-call | tf_op jit(solution)/shard_map/exchange/pallas_call | solution.py:221
  234.8 240.2 %expert.1 = (bf16[128,2048]{1,0:T(8,128)(2,1)}, bf16[128,2048]{1,0:T(8,128)(2,1)}, bf16[16,8,16,2048]{3,2,1,0:T(8,128)(2,1)}, bf16[16,8,16,2048]{3,2,1,0:T(8,128...) custom-call(bf16[16,8,16,2048]{3,2,1,0:T(8,128)(2,1)} %get-tuple-element.19.x, ...), custom_call_target="tpu_custom_call" | custom-call | tf_op jit(solution)/shard_map/expert/pallas_call | solution.py:525
  474.9 1.9 copy.17
  476.8 1.9 copy.18
  478.7 0.0 copy-start.1
  478.7 3.9 copy.19
  482.6 0.0 copy-done.1
  482.6 0.0 copy-start
  482.6 1.7 copy.20
  484.3 1.4 copy-done
  485.6 1.7 copy.21
  (3 shorter events, 0.0 us)
Async XLA Ops:
  478.7 3.9 copy-start.1
  482.6 3.0 copy-start

commit v4 on v3

--- a/solution.py
+++ b/solution.py
@@ -64,70 +64,64 @@
     )
 
 
-def gather_kernel(tok, meta, tok_all, meta_all, send, recv, fsend, frecv, local):
+def gather_kernel(meta, meta_all, send, recv, local):
     me = lax.axis_index("dp")
-    greet((2, 4, 6, 1), ())
-    pairs = ((meta, meta_all), (tok, tok_all))
-    copies = []
-    for i, (src, dst) in enumerate(pairs):
-        for n, step in enumerate((4, 2, 6, 1)):
-            copy = to_column(step, src, dst.at[me], send.at[i, n], recv.at[i, n])
-            copy.start()
-            copies.append(copy)
-    locals_ = []
-    for i, (src, dst) in enumerate(pairs):
-        copy = pltpu.make_async_copy(src, dst.at[me], local.at[i])
+    greet(COLUMN_STEPS, ())
+    copies = [
+        to_column(step, meta, meta_all.at[me], send.at[n], recv.at[n]) for n, step in enumerate(COLUMN_STEPS)
+    ]
+    copies.append(pltpu.make_async_copy(meta, meta_all.at[me], local))
+    for copy in copies:
         copy.start()
-        locals_.append(copy)
-    forwards = []
-    for i, (src, dst) in enumerate(pairs):
-        for n, step in ((1, 2), (2, 6), (0, 4)):
-            behind = column_peer(step)[1]
-            copies[4 * i + n].wait_recv()
-            copy = to_column(1, dst.at[behind], dst.at[behind], fsend.at[i, n], frecv.at[i, n])
-            copy.start()
-            forwards.append(copy)
-    for i in range(2):
-        copies[4 * i + 3].wait_recv()
     for copy in copies:
-        copy.wait_send()
-    for copy in forwards:
         copy.wait()
-    for copy in locals_:
-        copy.wait()
-
-
-def gather_column(tok, meta):
+
+
+def gather_column(meta):
     dma = pltpu.SemaphoreType.DMA
     return pl.pallas_call(
         gather_kernel,
-        out_shape=[
-            jax.ShapeDtypeStruct((DP,) + tok.shape, tok.dtype),
-            jax.ShapeDtypeStruct((DP,) + meta.shape, meta.dtype),
-        ],
-        in_specs=[ANY] * 2,
-        out_specs=[ANY] * 2,
-        scratch_shapes=[dma((2, 4)), dma((2, 4)), dma((2, 3)), dma((2, 3)), dma((2,))],
+        out_shape=jax.ShapeDtypeStruct((DP,) + meta.shape, meta.dtype),
+        in_specs=[ANY],
+        out_specs=ANY,
+        scratch_shapes=[dma((DP - 1,)), dma((DP - 1,)), dma],
         compiler_params=pltpu.CompilerParams(collective_id=0, has_side_effects=True),
         name="gather_column",
-    )(tok, meta)
+    )(meta)
 
 
 PEERS = EP - 1
 SENDS = DP * PEERS
 WINDOW = 24
-HALF = DP // 2
-
-
-def exchange_kernel(tok_all, grd, pick, weight, p, q, r, a_out, b_out, p_out, q_out, r_out,
-                    grd_all, tok_rows, grd_rows,
+
+
+def exchange_kernel(tok, grd, pick, weight, p, q, r, a_out, b_out, p_out, q_out, r_out,
+                    tok_all, grd_all, tok_rows, grd_rows,
                     psend, precv, csend, crecv, gsend, grecv, fsend, frecv, local):
     dp, ep = lax.axis_index("dp"), lax.axis_index("expert")
+    z, core = dp // 2, dp % 2
+    gathered = ((tok, tok_all), (grd, grd_all))
+
+    def place(j):
+        return (z + ((0b10110100 >> (j // 2 * 2)) & 3)) % SIDE * 2 + (core + j % 2) % 2
+
+    own = [
+        pltpu.make_async_copy(src, dst.at[dp], local.at[5 + i]) for i, (src, dst) in enumerate(gathered)
+    ]
+    own[0].start()
     greet(COLUMN_STEPS, PLANE_STEPS)
     gathers = [
-        to_column(step, grd, grd_all.at[dp], gsend.at[n], grecv.at[n]) for n, step in enumerate((4, 2, 6, 1))
+        [
+            to_column(step, src, dst.at[dp], gsend.at[i, n], grecv.at[i, n])
+            for n, step in enumerate((1, 6, 2, 4))
+        ]
+        for i, (src, dst) in enumerate(gathered)
     ]
-    own = pltpu.make_async_copy(grd, grd_all.at[dp], local.at[5])
+
+    def forward(i, m):
+        block = gathered[i][1].at[place(2 * m)]
+        return to_column(1, block, block, fsend.at[i, m - 1], frecv.at[i, m - 1])
+
     columns = []
     for n, step in enumerate(COLUMN_STEPS):
         target = column_peer(step)[0]
@@ -143,7 +137,7 @@
 
     def plane(i, k):
         src, dst = ends[i]
-        target, part = ordered_plane(k % PEERS)[0], k // PEERS
+        target, part = ordered_plane(k % PEERS)[0], place(k // PEERS)
         return pltpu.make_async_remote_copy(
             src_ref=src.at[target, part], dst_ref=dst.at[ep, part],
             send_sem=psend.at[i, k], recv_sem=precv.at[i, k],
@@ -156,40 +150,57 @@
             plane(i, k - WINDOW).wait_send()
             plane(i, k).start()
 
-    def spread(matrix, rows, result, start, stop):
-        @pl.loop(start, stop)
-        def _(source):
-            picked = dot(matrix[source], rows[source]).astype(BF16)
-            result[:, source] = picked.reshape(EP, CAP, picked.shape[-1])
-
-    for copy in gathers + [own]:
+    def spread(matrix, rows, result, j):
+        part = place(j)
+        picked = dot(matrix[part], rows[part]).astype(BF16)
+        result[:, part] = picked.reshape(EP, CAP, picked.shape[-1])
+
+    for copy in gathers[0] + gathers[1] + own[1:]:
         copy.start()
-    spread(pick, tok_all, tok_rows, 0, HALF)
-
-    @pl.loop(0, WINDOW)
-    def _(k):
-        plane(0, k).start()
-
-    spread(pick, tok_all, tok_rows, HALF, DP)
+    own[0].wait()
+    for m in range(SIDE):
+        if m:
+            gathers[0][m].wait_recv()
+            forward(0, m).start()
+        for j in (2 * m, 2 * m + 1):
+            if j == 1:
+                gathers[0][0].wait_recv()
+            elif j % 2:
+                forward(0, m).wait_recv()
+            spread(pick, tok_all, tok_rows, j)
+            if j == 0:
+
+                @pl.loop(0, PEERS)
+                def _(k):
+                    plane(0, k).start()
+
+            elif j == 1:
+
+                @pl.loop(PEERS, WINDOW)
+                def _(k):
+                    plane(0, k).start()
+
+                go_on(0, WINDOW, 2 * PEERS)
+            else:
+                go_on(0, j * PEERS, j * PEERS + (PEERS if j < DP - 1 else PEERS // 2))
+        if m == 2:
+            for n in range(1, SIDE):
+                gathers[1][n].wait_recv()
+                forward(1, n).start()
+            for copy in columns:
+                copy.start()
     own_rows[0].start()
-    go_on(0, WINDOW, 56)
-    forwards = []
-    for n, step in ((1, 2), (2, 6), (0, 4)):
-        behind = column_peer(step)[1]
-        gathers[n].wait_recv()
-        copy = to_column(1, grd_all.at[behind], grd_all.at[behind], fsend.at[n], frecv.at[n])
-        copy.start()
-        forwards.append(copy)
-    for copy in columns:
-        copy.start()
-    go_on(0, 56, 100)
-    gathers[3].wait_recv()
-    for copy in forwards:
-        copy.wait_recv()
-    own.wait()
-    spread(weight, grd_all, grd_rows, 0, DP)
+    gathers[1][0].wait_recv()
+    own[1].wait()
+    for n in range(1, SIDE):
+        forward(1, n).wait_recv()
+
+    @pl.loop(0, DP)
+    def _(j):
+        spread(weight, grd_all, grd_rows, j)
+
     own_rows[1].start()
-    go_on(0, 100, SENDS)
+    go_on(0, SENDS - PEERS + PEERS // 2, SENDS)
 
     @pl.loop(0, WINDOW)
     def _(k):
@@ -208,33 +219,37 @@
         def _(k):
             plane(i, k).wait_recv()
 
-    for copy in gathers + forwards:
-        copy.wait_send()
+    for i in range(2):
+        for copy in gathers[i]:
+            copy.wait_send()
+        for m in range(1, SIDE):
+            forward(i, m).wait_send()
     for copy in columns + own_rows:
         copy.wait()
 
 
-def exchange(tok_all, grd, pick, weight, p, q, r):
+def exchange(tokens, grd, pick, weight, p, q, r):
     tok, width = grd.shape
     dma = pltpu.SemaphoreType.DMA
     rows = (EP, DP, CAP, width)
     return pl.pallas_call(
         exchange_kernel,
         out_shape=[jax.ShapeDtypeStruct(rows, BF16)] * 2 + [jax.ShapeDtypeStruct(p.shape, BF16)] * 3,
-        in_specs=[VMEM, ANY, VMEM, VMEM, ANY, ANY, ANY],
+        in_specs=[ANY, ANY, VMEM, VMEM, ANY, ANY, ANY],
         out_specs=[ANY] * 5,
         scratch_shapes=[
+            pltpu.VMEM((DP, tok, width), BF16),
             pltpu.VMEM((DP, tok, width), BF16),
             pltpu.VMEM(rows, BF16),
             pltpu.VMEM(rows, BF16),
             dma((2, SENDS)), dma((2, SENDS)), dma((3, DP - 1)), dma((3, DP - 1)),
-            dma((4,)), dma((4,)), dma((3,)), dma((3,)), dma((6,)),
+            dma((2, SIDE)), dma((2, SIDE)), dma((2, SIDE - 1)), dma((2, SIDE - 1)), dma((7,)),
         ],
         compiler_params=pltpu.CompilerParams(
             collective_id=1, has_side_effects=True, vmem_limit_bytes=63 * 2**20
         ),
         name="exchange",
-    )(tok_all, grd, pick, weight, p, q, r)
+    )(tokens, grd, pick, weight, p, q, r)
 
 
 NT = (((1,), (1,)), ((), ()))
@@ -416,11 +431,11 @@
             rg_v[source] = rg[these].reshape(DP, CAP, -1)
             held = pl.ds(pl.multiple_of(source * ROWS, ROWS), ROWS)
             hid[held], gg[held], ug[held] = hidden[these], gate_grad[these], up_grad[these]
-        @pl.loop(0, 12)
+        @pl.loop(0, 10)
         def _(j):
-            back(0, n * 12 + j).start()
-
-    first = 12 * groups
+            back(0, n * 10 + j).start()
+
+    first = 10 * groups
 
     for i in range(2):
         own_back(i).start()
@@ -454,11 +469,11 @@
             for copy in own_grads():
                 copy.start()
 
-        @pl.when(n < (SENDS - first) // 4)
-        def _():
-            for j in range(4):
-                back(0, first - WINDOW + 4 * n + j).wait_send()
-                back(0, first + 4 * n + j).start()
+        @pl.loop(0, (SENDS - first) // DP)
+        def _(j):
+            k = first + n * ((SENDS - first) // DP) + j
+            back(0, k - WINDOW).wait_send()
+            back(0, k).start()
 
     @pl.loop(0, WINDOW)
     def _(k):
@@ -555,7 +570,7 @@
     tok, width = tokens.shape
     ff = w_gate.shape[-1]
     meta = (expert_ids * 256 + gate_codes).T
-    tok_all, meta_all = gather_column(tokens, meta)
+    meta_all = gather_column(meta)
     ids, codes = meta_all // 256, meta_all % 256
     mine = jnp.arange(EP, dtype=jnp.int32) * DP + dp
     named = ids[:, None] == mine[None, :, None, None]
@@ -567,7 +582,7 @@
     pick = slot == jnp.arange(CAP, dtype=jnp.int32)[None, None, :, None]
     weight = jnp.where(pick, gate[:, :, None, :], 0.0).astype(BF16).reshape(DP, EP * CAP, tok)
     pick = pick.astype(BF16).reshape(DP, EP * CAP, tok)
-    x, u, wg, wu, wd = exchange(tok_all, grad_out, pick, weight, w_gate, w_up, w_down)
+    x, u, wg, wu, wd = exchange(tokens, grad_out, pick, weight, w_gate, w_up, w_down)
     wg, wu, wd = (w.reshape(width, ff) for w in (wg, wu, wd))
     return expert(x, u, wg, wu, wd, weight, pick)
 

time: 495 us -> 487 us (0.984)
  Pallas kernels: 469 us -> 461 us
    pallas_call x1, Pallas kernels: 32.7 us -> 7.91 us  [gather_column(): pl.pallas_call(gather_kernel, out_shape=jax.ShapeDtypeStruct((DP,) + meta...]
    pallas_call x1, Pallas kernels: 240 us -> 259 us  [expert(): pl.pallas_call(expert_kernel, out_shape=[jax.ShapeDtypeStruct((tok, width...]
where the time goes in v4:
time: 487 us; the launch traced here: 479 us
  Pallas kernels  461 us (95%)
  local copies, waits for them, and re-layouts  12.4 us (3%)
    pallas_call x1, Pallas kernels, expert(): pl.pallas_call(expert_kernel, out_shape=[jax.ShapeDtypeStruct((tok, width...  259 us
    pallas_call x1, Pallas kernels, exchange(): pl.pallas_call(exchange_kernel, out_shape=[jax.ShapeDtypeStruct(rows, BF1...  194 us
    unnamed x9, local copies, waits for them, and re-layouts  12.4 us

profile of v4, /device:TPU:3, one launch (start us, length us, event | category | flops | bytes accessed | tf_op | source)
XLA Modules:
  0.0 478.7 jit_solution(16627111726683007872)
XLA Ops:
  0.6 1.3 add_bitcast_fusion.meta
  2.0 0.1 eq.42
  2.0 7.9 %gather_column.1 = s32[8,8,128]{2,1,0:T(8,128)} custom-call(s32[8,128]{1,0:T(8,128)} %add_bitcast_fusion.meta), custom_call_target="tpu_custom_call" | custom-call | tf_op jit(solution)/shard_map/gather_column/pallas_call | solution.py:82
  9.9 0.8 add_select_fusion
  10.7 0.2 compare_reduce_fusion
  11.0 0.2 fusion.3
  11.2 0.1 fusion
  11.4 1.0 fusion.1.weight
  12.4 1.0 fusion.2.pick
  13.3 194.0 %exchange.1 = (bf16[16,8,16,2048]{3,2,1,0:T(8,128)(2,1)}, bf16[16,8,16,2048]{3,2,1,0:T(8,128)(2,1)}, bf16[8,256,768]{2,1,0:T(8,128)(2,1)}, bf16[8,256,768]{2,1,0:T(8,128)(2,1)}, bf16[8,256,768]{2,1,0:T(8,128)(2,1)}) custom-call(bf16[128,2048]{1,0:T(8,128)(2,1)} %tok.1, bf16[128,2048]{1,0:T(8,128)(2,1)} %grd.1, bf16[8,256,128]{2,1,0:T(8,128)(2,1)} %fusion.2.pick, ...), custom_call_target="tpu_custom_call" | custom-call | tf_op jit(solution)/shard_map/exchange/pallas_call | solution.py:235
  207.4 259.0 %expert.1 = (bf16[128,2048]{1,0:T(8,128)(2,1)}, bf16[128,2048]{1,0:T(8,128)(2,1)}, bf16[16,8,16,2048]{3,2,1,0:T(8,128)(2,1)}, bf16[16,8,16,2048]{3,2,1,0:T(8,128...) custom-call(bf16[16,8,16,2048]{3,2,1,0:T(8,128)(2,1)} %get-tuple-element.15.x, ...), custom_call_target="tpu_custom_call" | custom-call | tf_op jit(solution)/shard_map/expert/pallas_call | solution.py:540
  466.4 1.9 copy.17
  468.2 1.9 copy.18
  470.1 0.0 copy-start.1
  470.1 3.9 copy.19
  474.0 0.0 copy-done.1
  474.0 0.0 copy-start
  474.0 1.7 copy.20
  475.7 1.4 copy-done
  477.1 1.7 copy.21
  (3 shorter events, 0.0 us)
Async XLA Ops:
  470.1 3.9 copy-start.1
  474.0 3.0 copy-start

commit v5 on v4

--- a/solution.py
+++ b/solution.py
@@ -431,11 +431,11 @@
             rg_v[source] = rg[these].reshape(DP, CAP, -1)
             held = pl.ds(pl.multiple_of(source * ROWS, ROWS), ROWS)
             hid[held], gg[held], ug[held] = hidden[these], gate_grad[these], up_grad[these]
-        @pl.loop(0, 10)
+        @pl.loop(0, 12)
         def _(j):
-            back(0, n * 10 + j).start()
-
-    first = 10 * groups
+            back(0, n * 12 + j).start()
+
+    first = 12 * groups
 
     for i in range(2):
         own_back(i).start()
@@ -469,11 +469,11 @@
             for copy in own_grads():
                 copy.start()
 
-        @pl.loop(0, (SENDS - first) // DP)
-        def _(j):
-            k = first + n * ((SENDS - first) // DP) + j
-            back(0, k - WINDOW).wait_send()
-            back(0, k).start()
+        @pl.when(n < (SENDS - first) // 4)
+        def _():
+            for j in range(4):
+                back(0, first - WINDOW + 4 * n + j).wait_send()
+                back(0, first + 4 * n + j).start()
 
     @pl.loop(0, WINDOW)
     def _(k):

time: 487 us -> 480 us (0.986)
  Pallas kernels: 461 us -> 452 us
    pallas_call x1, Pallas kernels: 259 us -> 250 us  [expert(): pl.pallas_call(expert_kernel, out_shape=[jax.ShapeDtypeStruct((tok, width...]
where the time goes in v5:
time: 480 us; the launch traced here: 470 us
  Pallas kernels  452 us (94%)
  local copies, waits for them, and re-layouts  12.4 us (3%)
    pallas_call x1, Pallas kernels, expert(): pl.pallas_call(expert_kernel, out_shape=[jax.ShapeDtypeStruct((tok, width...  250 us
    pallas_call x1, Pallas kernels, exchange(): pl.pallas_call(exchange_kernel, out_shape=[jax.ShapeDtypeStruct(rows, BF1...  194 us
    unnamed x9, local copies, waits for them, and re-layouts  12.4 us

profile of v5, /device:TPU:3, one launch (start us, length us, event | category | flops | bytes accessed | tf_op | source)
XLA Modules:
  0.0 470.2 jit_solution(14041043086984787967)
XLA Ops:
  0.6 1.3 add_bitcast_fusion.meta
  2.0 0.1 eq.42
  2.0 7.9 %gather_column.1 = s32[8,8,128]{2,1,0:T(8,128)} custom-call(s32[8,128]{1,0:T(8,128)} %add_bitcast_fusion.meta), custom_call_target="tpu_custom_call" | custom-call | tf_op jit(solution)/shard_map/gather_column/pallas_call | solution.py:82
  9.9 0.8 add_select_fusion
  10.7 0.2 compare_reduce_fusion
  11.0 0.2 fusion.3
  11.2 0.1 fusion
  11.4 1.0 fusion.1.weight
  12.4 1.0 fusion.2.pick
  13.3 194.0 %exchange.1 = (bf16[16,8,16,2048]{3,2,1,0:T(8,128)(2,1)}, bf16[16,8,16,2048]{3,2,1,0:T(8,128)(2,1)}, bf16[8,256,768]{2,1,0:T(8,128)(2,1)}, bf16[8,256,768]{2,1,0:T(8,128)(2,1)}, bf16[8,256,768]{2,1,0:T(8,128)(2,1)}) custom-call(bf16[128,2048]{1,0:T(8,128)(2,1)} %tok.1, bf16[128,2048]{1,0:T(8,128)(2,1)} %grd.1, bf16[8,256,128]{2,1,0:T(8,128)(2,1)} %fusion.2.pick, ...), custom_call_target="tpu_custom_call" | custom-call | tf_op jit(solution)/shard_map/exchange/pallas_call | solution.py:235
  207.4 250.4 %expert.1 = (bf16[128,2048]{1,0:T(8,128)(2,1)}, bf16[128,2048]{1,0:T(8,128)(2,1)}, bf16[16,8,16,2048]{3,2,1,0:T(8,128)(2,1)}, bf16[16,8,16,2048]{3,2,1,0:T(8,128...) custom-call(bf16[16,8,16,2048]{3,2,1,0:T(8,128)(2,1)} %get-tuple-element.15.x, ...), custom_call_target="tpu_custom_call" | custom-call | tf_op jit(solution)/shard_map/expert/pallas_call | solution.py:540
  457.8 1.9 copy.17
  459.7 1.9 copy.18
  461.6 0.0 copy-start.1
  461.6 3.9 copy.19
  465.5 0.0 copy-done.1
  465.5 0.0 copy-start
  465.5 1.7 copy.20
  467.2 1.4 copy-done
  468.5 1.7 copy.21
  (3 shorter events, 0.0 us)
Async XLA Ops:
  461.6 3.9 copy-start.1
  465.5 3.0 copy-start
